TPU v7x, 256 devices: a whole 4x4x8 slice. The times are simulated.
256 devices in a mesh: replica: 8 (over x_hi, y), shard: 32 (over x_lo, z, core).
Axes of the slice: x: 4 (x_hi: 2, x_lo: 2; x = x_hi * 2 + x_lo), y: 4, z: 8, core: 2. Of those that a mesh axis runs over, the one named last changes fastest.
Arguments:
- tokens: bfloat16 [32768, 8192], P(('replica', 'shard')), may hold values from -24 to 24
- cotangent: bfloat16 [32768, 512], P(('replica', 'shard')), may hold values from -6 to 6
- base_copy: bfloat16 [8192, 512], replicated, may hold values from -0.0625 to 0.0625
- codes: int32 [8192, 512], P('shard'), may hold values from -8 to 7
- scales: float32 [8192, 4], P('shard'), may hold values from 0.001 to 0.004
Outputs:
- projected: bfloat16 [32768, 512], P(('replica', 'shard'))
- input_grad: bfloat16 [32768, 8192], P(('replica', 'shard'))
- weight_grad: float32 [8192, 512], P('shard')
All inputs are finite; a program needn't handle non-finite values.
Results may differ from a plain program's by a relative error of at most 0.0055.
Values may be sent and summed in bfloat16 or wider, within the bound.
A program may use at most 128 MiB of HBM per device.

v0:
```python
import math

import jax
import jax.numpy as jnp
from jax import lax
from jax.sharding import PartitionSpec as P


def body(tokens, cotangent, base_copy, codes, scales):
    rows, width = codes.shape
    groups = scales.shape[1]
    replicas = lax.axis_size("replica")
    shards = lax.axis_size("shard")
    tok_count = tokens.shape[0]
    factor = 1.0 / math.sqrt(tok_count * replicas * shards)
    difference = (
        (codes.astype(jnp.float32).reshape(rows, groups, width // groups) * scales[:, :, None])
        .reshape(rows, width)
        .astype(jnp.bfloat16)
    )
    weight = (
        base_copy.astype(jnp.float32)
        + lax.all_gather(difference, "shard", axis=0, tiled=True).astype(jnp.float32)
    ).astype(jnp.bfloat16)
    columns = tokens
    out_acc = jnp.dot(columns, weight, preferred_element_type=jnp.float32)
    back_block = lax.dot_general(
        cotangent, weight, (((1,), (1,)), ((), ())), preferred_element_type=jnp.float32
    )
    back_acc = back_block
    out_acc, back_acc = (out_acc, back_acc)
    projected = out_acc.astype(jnp.bfloat16)
    input_grad = back_acc.astype(jnp.bfloat16)
    columns = tokens
    shard_sum = lax.psum_scatter(
        lax.dot_general(
            columns, cotangent, (((0,), (0,)), ((), ())), preferred_element_type=jnp.float32
        )
        * factor,
        "shard",
        scatter_dimension=0,
        tiled=True,
    )
    weight_grad = lax.psum(shard_sum, "replica")
    return (projected, input_grad, weight_grad)


def solution(mesh):
    return jax.shard_map(
        body,
        mesh=mesh,
        in_specs=(
            P(("replica", "shard"), None),
            P(("replica", "shard"), None),
            P(),
            P("shard", None),
            P("shard", None),
        ),
        out_specs=(P(("replica", "shard"), None), P(("replica", "shard"), None), P("shard", None)),
        check_vma=False,
    )
```

profile of v0, /device:TPU:1, one launch (start us, length us, event | category | flops | bytes accessed | tf_op | source)
XLA Modules:
  0.0 325.1 jit_solution(16563144663611239408)
XLA Ops:
  7.2 0.0 copy-start
  7.2 0.0 all-gather.2.cloned.1.call-start
  7.2 1.0 copy.8
  8.2 0.3 mul.17
  8.5 1.9 fusion.4
  10.4 0.0 all-gather.2.cloned.1.call-update
  10.4 0.0 reduce-scatter.2.cloned.1.call-start
  10.4 0.0 copy-done
  10.5 9.0 %convolution_multiply_fusion = f32[8192,512]{1,0:T(8,128)} fusion(bf16[128,8192]{1,0:T(8,128)(2,1)S(1)} %copy-done, bf16[128,512]{1,0:T(8,128)(2,1)} %param.6), kind=kOutput, calls=%fused_computation.1 | convolution fusion | flops 1077936128 | bytes 19005440 | tf_op jit(solution)/shard_map/dot_general | solution.py:36
  19.4 0.0 reduce-scatter.2.cloned.1.call-update
  19.5 0.0 copy-start.1
  19.5 0.0 all-reduce.2.cloned.1.call-start
  19.5 67.5 %all-gather.2.cloned.1.call-done = bf16[8192,512]{1,0:T(8,128)(2,1)} async-done(((bf16[256,512]{1,0:T(8,128)(2,1)}), bf16[8192,512]{1,0:T(8,128)(2,1)}) %all-gather.2.cloned.1.call-update) | async-done | bytes 8388624 | tf_op jit(solution)/shard_map/all_gather | solution.py:23
  87.1 8.2 %fusion.3 = bf16[128,512]{0,1:T(8,128)(2,1)S(1)} fusion(bf16[128,8192]{1,0:T(8,128)(2,1)S(1)} %copy-done, bf16[8192,512]{1,0:T(8,128)(2,1)} %all-gather.2.cloned.1.call-done, bf16[8192,512]{1,0:T(8,128)(2,1)} %param.7), kind=kOutput, calls=%fused_computation.6 | convolution fusion | flops 1090584576 | bytes 19005440 | tf_op jit(solution)/shard_map/dot_general | solution.py:26
  95.2 134.5 %reduce-scatter.2.cloned.1.call-done = f32[256,512]{1,0:T(8,128)} async-done(((f32[8192,512]{1,0:T(8,128)}), f32[256,512]{1,0:T(8,128)}) %reduce-scatter.2.cloned.1.call-update) | async-done | bytes 524304 | tf_op jit(solution)/shard_map/reduce_scatter | solution.py:35
  229.7 0.0 all-reduce.2.cloned.1.call-update
  229.7 0.0 copy-done.1
  229.7 9.5 %fusion = bf16[128,8192]{0,1:T(8,128)(2,1)} fusion(bf16[128,512]{1,0:T(8,128)(2,1)S(1)} %copy-done.1, bf16[8192,512]{1,0:T(8,128)(2,1)} %all-gather.2.cloned.1.call-done, bf16[8192,512]{1,0:T(8,128)(2,1)} %param.7), kind=kOutput, calls=%fused_computation.3 | convolution fusion | flops 1091567616 | bytes 19005440 | tf_op jit(solution)/shard_map/dot_general | solution.py:27
  239.2 4.1 %copy.10 = bf16[128,8192]{1,0:T(8,128)(2,1)} copy(bf16[128,8192]{0,1:T(8,128)(2,1)} %fusion) | data formatting | bytes 4194304
  243.3 0.8 copy.9
  244.0 72.6 %all-reduce.2.cloned.1.call-done = f32[256,512]{1,0:T(8,128)} async-done(((f32[256,512]{1,0:T(8,128)}), f32[256,512]{1,0:T(8,128)}) %all-reduce.2.cloned.1.call-update) | async-done | bytes 524304 | tf_op jit(solution)/shard_map/psum | solution.py:44
  316.7 1.9 copy.14
Async XLA Ops:
  7.2 3.3 %copy-start = (bf16[128,8192]{1,0:T(8,128)(2,1)S(1)}, bf16[128,8192]{1,0:T(8,128)(2,1)}, u32[]{:S(2)}) copy-start(bf16[128,8192]{1,0:T(8,128)(2,1)} %param.5) | copy-start | bytes 6291460
  7.2 79.9 %all-gather.2.cloned.1.call-start = ((), (), s32[]{:S(2)}) async-start(), calls=%async_computation.1 | async-start | bytes 8650752 | tf_op jit(solution)/shard_map/all_gather | solution.py:23
  10.4 219.3 %reduce-scatter.2.cloned.1.call-start = ((), (), s32[]{:S(2)}) async-start(), calls=%async_computation.2 | async-start | bytes 17301504 | tf_op jit(solution)/shard_map/reduce_scatter | solution.py:35
  19.5 210.3 %copy-start.1 = (bf16[128,512]{1,0:T(8,128)(2,1)S(1)}, bf16[128,512]{1,0:T(8,128)(2,1)}, u32[]{:S(2)}) copy-start(bf16[128,512]{1,0:T(8,128)(2,1)} %param.6) | copy-start | bytes 393220
  19.5 297.2 %all-reduce.2.cloned.1.call-start = ((), (), s32[]{:S(2)}) async-start(), calls=%async_computation.3 | async-start | bytes 1048576 | tf_op jit(solution)/shard_map/psum | solution.py:44
Sparse Core Ops, SparseCore 0:
  10.5 76.4 all-gather.1
  89.6 140.0 reduce-scatter.1
  232.3 84.3 all-reduce.1
where the time goes:
time: 330 us; the launch traced here: 325 us
  waiting for transfers between devices  275 us (83%)
  matrix products  26.6 us (8%)
  between operations  13.8 us (4%)
  local copies, waits for them, and re-layouts  8 us (2%)
    reduce_scatter x1, waiting for transfers between devices, body(): lax.psum_scatter(lax.dot_general(columns, cotangent, (((0,), (0,)), ((),...  134 us
    psum x1, waiting for transfers between devices, body(): weight_grad = lax.psum(shard_sum, 'replica')  72.6 us
    all_gather x1, waiting for transfers between devices, body(): lax.all_gather(difference, 'shard', axis=0, tiled=True).astype(jnp.float32)  67.5 us
    dot_general x1, matrix products, body(): lax.dot_general(cotangent, weight, (((1,), (1,)), ((), ())), preferred_el...  9.48 us
    dot_general x1, matrix products, body(): lax.dot_general(columns, cotangent, (((0,), (0,)), ((), ())), preferred_e...  8.98 us
    dot_general x1, matrix products, body(): out_acc = jnp.dot(columns, weight, preferred_element_type=jnp.float32)  8.17 us
    unnamed x8, local copies, waits for them, and re-layouts  7.67 us
  transfers between devices with their start and end apart: 3, of which 3 were waited for; matrix products, arithmetic and copies ran while one was open for 10% of the time, Pallas kernels for 0%

commit v1 on v0

v1 whole, which is shorter than its diff:
```python
import math

import jax
import jax.numpy as jnp
from jax import lax
from jax.experimental import pallas as pl
from jax.experimental.pallas import tpu as pltpu
from jax.sharding import PartitionSpec as P

BF16 = jnp.bfloat16
F32 = jnp.float32


def kernel(
    tok, cot, base, codes, scales,
    proj, igrad, wgrad,
    W, BASE, TK, CA, TW, GF, GX, XR, ZS, ZR, RB, RR, IG, PA, PR, CO, SC,
    ld, tk_l, tk_s, tk_r, ca_s, ca_r, tw_s, tw_r, az_s, az_r, ax_s, ax_r,
    ig_l, ig_s, ig_r, gx_s, gx_r, zs_s, zs_r, rr_s, rr_r, pa_s, pa_r,
):
    r = lax.axis_index("replica")
    s = lax.axis_index("shard")
    X, y = r // 4, r % 4
    l, z, c = s // 16, (s % 16) // 2, s % 2
    oc = 1 - c

    def dev(X=X, y=y, l=l, z=z, c=c):
        return {"replica": X * 4 + y, "shard": l * 16 + z * 2 + c}

    up, down = dev(z=(z + 1) % 8), dev(z=(z + 7) % 8)
    A, B, O = dev(l=1 - l), dev(X=1 - X, l=1 - l), dev(X=1 - X)
    peer = dev(c=oc)

    def wait(ref, sem):
        pltpu.make_async_copy(ref, ref, sem).wait()

    def send(src, dst, ssem, rsem, to):
        pltpu.make_async_remote_copy(src, dst, ssem, rsem, device_id=to).start()

    pltpu.make_async_copy(codes, CO, ld.at[0]).start()
    pltpu.make_async_copy(scales, SC, ld.at[1]).start()
    me8 = y * 2 + c
    pltpu.make_async_copy(cot, CA.at[me8], ca_r.at[me8]).start()

    barrier = pltpu.get_barrier_semaphore()
    peers = [peer]
    peers += [dev(y=(y + d) % 4, c=cc) for d in (1, 2, 3) for cc in (c, oc)]
    peers += [dev(z=(z + d) % 8) for d in range(1, 8)]
    peers += [A, B, O]
    peers += [dev(X=1 - X, y=(y + d) % 4) for d in (1, 2, 3)]
    for d in peers:
        pl.semaphore_signal(barrier, 1, device_id=d)

    def col(block, core):
        return pl.multiple_of((block * 2 + core) * 256, 256)

    def load_block(b, _):
        rows = pl.ds(col(b, c), 256)
        pltpu.make_async_copy(base.at[rows], BASE.at[b], ld.at[2]).start()
        dst = pl.ds(pl.multiple_of(b * 256, 256), 256)
        pltpu.make_async_copy(
            tok.at[:, rows], TK.at[pl.ds(c * 128, 128), dst], tk_l
        ).start()
        return 0

    lax.fori_loop(0, 16, load_block, 0)

    wait(CO, ld.at[0])
    wait(SC, ld.at[1])
    own = l * 8 + z
    for g in range(4):
        lanes = pl.ds(g * 128, 128)
        W[own, :, lanes] = (CO[:, lanes].astype(F32) * SC[:, g : g + 1]).astype(BF16)

    pl.semaphore_wait(barrier, len(peers))

    def half(block, h):
        return W.at[block, pl.ds(h * 128, 128)]

    def send_z(block, t, way, h):
        send(half(block, h), half(block, h), az_s, az_r.at[t, way, h], (up, down)[way])

    def send_x(block, zz, h):
        send(half(block, h), half(block, h), ax_s, ax_r.at[zz, h], (A, B)[h])

    for h in range(2):
        send_z(own, 0, 0, h)
        send_z(own, 0, 1, h)
        send_x(own, z, h)

    send(cot, CA.at[me8], ca_s, ca_r.at[me8], peer)
    for d in (1, 3, 2):
        send(cot, CA.at[me8], ca_s, ca_r.at[me8], dev(y=(y + d) % 4))

    def send_tokens(b, _):
        src = pl.ds(col(b, oc), 256)
        dst = pl.ds(pl.multiple_of(b * 256, 256), 256)
        send(tok.at[:, src], TK.at[pl.ds(c * 128, 128), dst], tk_s, tk_r, peer)
        return 0

    lax.fori_loop(0, 16, send_tokens, 0)

    my_rows = pl.ds(pl.multiple_of(me8 * 128, 128), 128)

    def kof(i):
        return lax.rem(z // 2 + i + 1, 4)

    def chunk(p, i, j, core):
        return pl.multiple_of(
            ((p * 8 + 2 * kof(i) + j % 2) * 2 + core) * 256 + (j // 2) * 128, 128
        )

    def send_part(i):
        for p in range(2):
            dst = TW.at[i, my_rows, pl.ds(p * 128, 128)]
            pltpu.make_async_copy(
                tok.at[:, pl.ds(chunk(p, i, y, c), 128)], dst, tw_r.at[i]
            ).start()
            for d in (1, 3, 2, 0):
                j = (y + d) % 4
                for cc in (c, oc):
                    if d == 0 and cc is c:
                        continue
                    send(
                        tok.at[:, pl.ds(chunk(p, i, j, cc), 128)], dst, tw_s, tw_r.at[i],
                        dev(y=j, c=cc),
                    )

    send_part(0)
    send_part(1)

    PA[...] = jnp.zeros_like(PA)
    wait(CA.at[me8], ca_r.at[me8])
    wait(CA.at[y * 2 + oc], ca_r.at[y * 2 + oc])
    wait(BASE, ld.at[2])
    half_tokens = TK.at[pl.ds(0, 128)]
    wait(half_tokens, tk_l)
    wait(half_tokens, tk_r)

    def offset(m):
        return jnp.where(m % 2 == 1, 8 - (m + 1) // 2, m // 2)

    def use_block(other, m):
        zz = lax.rem(z + offset(m), 8)
        block = jnp.where(other, (1 - l) * 8 + zz, l * 8 + zz)

        @pl.when(other)
        def _():
            for h in range(2):
                wait(half(block, h), ax_r.at[zz, h])

        w = (BASE[block].astype(F32) + W[block].astype(F32)).astype(BF16)
        lanes = pl.ds(pl.multiple_of(block * 256, 256), 256)
        PA[...] += jnp.dot(TK[:, lanes], w, preferred_element_type=F32)
        both = CA[pl.ds(y * 2, 2)].reshape(256, 512)
        IG[block] = lax.dot_general(
            both, w, (((1,), (1,)), ((), ())), preferred_element_type=F32
        ).astype(BF16)
        out = igrad.at[:, pl.ds(col(block, c), 256)]
        mine = IG.at[block, pl.ds(pl.multiple_of(c * 128, 128), 128)]
        theirs = IG.at[block, pl.ds(pl.multiple_of(oc * 128, 128), 128)]
        send(theirs, out, ig_s, ig_r, peer)
        pltpu.make_async_copy(mine, out, ig_l).start()

    def piece(p, half_x):
        return pl.multiple_of(p * 128 + half_x * 64, 64)

    def x_sum(i):
        wait(XR.at[i], gx_r.at[i])
        total = GF[pl.ds(piece(l, X), 64), :]
        for q in range(3):
            total = total + XR[i, q].astype(F32)
        ZS[i] = total.astype(BF16)
        to = 2 * kof(i) + y % 2

        @pl.when(to != z)
        def _():
            send(ZS.at[i], ZR.at[z], zs_s, zs_r, dev(z=to))

        @pl.when(to == z)
        def _():
            ZR[z] = total.astype(BF16)

    def part(i):
        @pl.when(i == 0)
        def _():
            for d in (1, 3, 2):
                k = ((y + d) % 4) * 2 + c
                wait(CA.at[k], ca_r.at[k])
                send(CA.at[k], CA.at[k], ca_s, ca_r.at[k], peer)
            for d in (1, 3, 2):
                k = ((y + d) % 4) * 2 + oc
                wait(CA.at[k], ca_r.at[k])

        wait(TW.at[i], tw_r.at[i])
        GF[...] = lax.dot_general(
            TW[i], CA[...].reshape(1024, 512), (((0,), (0,)), ((), ())),
            preferred_element_type=F32,
        )
        GX[i] = GF[...].astype(BF16)
        for q, (p, hx, to) in enumerate(((1 - l, X, A), (1 - l, 1 - X, B), (l, 1 - X, O))):
            send(GX.at[i, pl.ds(piece(p, hx), 64)], XR.at[i, q], gx_s, gx_r.at[i], to)

    def step(i, _):
        @pl.when(i < 4)
        def _():
            t = i
            zu, zd = lax.rem(z + 7 - t, 8), lax.rem(z + t + 1, 8)
            for h in range(2):
                for way, zz in ((0, zu), (1, zd)):
                    block = l * 8 + zz

                    @pl.when(jnp.logical_or(t < 3, h == way))
                    def _():
                        wait(half(block, h), az_r.at[t, way, h])

                        @pl.when(jnp.logical_or(t < 2, jnp.logical_and(t == 2, h == way)))
                        def _():
                            send_z(block, t + 1, way, h)

                        send_x(block, zz, h)

        @pl.when(i < 2)
        def _():
            send_part(i + 2)

        lo1 = jnp.where(i == 0, 0, jnp.minimum(2 * i + 1, 8))
        hi1 = jnp.minimum(2 * i + 3, 8)
        lo2 = jnp.maximum(2 * i - 1, 0)
        hi2 = jnp.minimum(2 * i + 1, 8)
        n1 = hi1 - lo1

        def one(n, _):
            other = n >= n1
            use_block(other, jnp.where(other, lo2 + n - n1, lo1 + n))
            return 0

        lax.fori_loop(0, n1 + hi2 - lo2, one, 0)

        @pl.when(i == 4)
        def _():
            send(PA.at[pl.ds(pl.multiple_of(oc * 128, 128), 128)], PR, pa_s, pa_r, peer)

        @pl.when(i > 0)
        def _():
            x_sum(i - 1)

        @pl.when(i < 4)
        def _():
            part(i)

        return 0

    lax.fori_loop(0, 5, step, 0)

    holds = z % 2 == y % 2
    slot = (y // 2) * 2 + X

    @pl.when(holds)
    def _():
        wait(ZR.at[pl.ds(0, 7)], zs_r)
        total = ZR[0].astype(F32)
        for q in range(1, 8):
            total = total + ZR[q].astype(F32)
        total = (total * (1.0 / math.sqrt(32768.0))).astype(BF16)
        RB[...] = total
        for XX in (X, 1 - X):
            for d in (1, 2, 3, 0):
                if XX is X and d == 0:
                    continue
                send(RB, RR.at[slot], rr_s, rr_r, dev(X=XX, y=(y + d) % 4))
        RR[slot] = total

    wait(PR, pa_r)
    proj[...] = (PA[pl.ds(pl.multiple_of(c * 128, 128), 128), :] + PR[...]).astype(BF16)

    @pl.when(holds)
    def _():
        wait(RR.at[pl.ds(0, 3)], rr_r)

    @pl.when(jnp.logical_not(holds))
    def _():
        wait(RR, rr_r)

    for q in range(4):
        wgrad[pl.ds(q * 64, 64), :] = RR[q].astype(F32)

    wait(half_tokens, tk_s)
    wait(CA.at[pl.ds(0, 7)], ca_s)
    wait(TW.at[:, pl.ds(0, 896)], tw_s)
    wait(W.at[pl.ds(0, 7)], az_s)
    wait(W.at[pl.ds(0, 8)], ax_s)
    wait(XR, gx_s)
    wait(PR, pa_s)

    @pl.when(holds)
    def _():
        wait(ZS.at[pl.ds(0, 3)], zs_s)
        wait(ZR.at[pl.ds(0, 7)], rr_s)

    @pl.when(jnp.logical_not(holds))
    def _():
        wait(ZS, zs_s)

    wait(half_tokens, ig_s)
    wait(half_tokens, ig_l)
    wait(half_tokens, ig_r)


def body(tokens, cotangent, base_copy, codes, scales):
    dma = pltpu.SemaphoreType.DMA
    anywhere = pl.BlockSpec(memory_space=pl.ANY)
    return pl.pallas_call(
        kernel,
        out_shape=(
            jax.ShapeDtypeStruct((128, 512), BF16),
            jax.ShapeDtypeStruct((128, 8192), BF16),
            jax.ShapeDtypeStruct((256, 512), F32),
        ),
        in_specs=[anywhere] * 5,
        out_specs=(
            pl.BlockSpec(memory_space=pltpu.VMEM),
            anywhere,
            pl.BlockSpec(memory_space=pltpu.VMEM),
        ),
        scratch_shapes=[
            pltpu.VMEM((16, 256, 512), BF16),
            pltpu.VMEM((16, 256, 512), BF16),
            pltpu.VMEM((256, 4096), BF16),
            pltpu.VMEM((8, 128, 512), BF16),
            pltpu.VMEM((4, 1024, 256), BF16),
            pltpu.VMEM((256, 512), F32),
            pltpu.VMEM((4, 256, 512), BF16),
            pltpu.VMEM((4, 3, 64, 512), BF16),
            pltpu.VMEM((4, 64, 512), BF16),
            pltpu.VMEM((8, 64, 512), BF16),
            pltpu.VMEM((64, 512), BF16),
            pltpu.VMEM((4, 64, 512), BF16),
            pltpu.VMEM((16, 256, 256), BF16),
            pltpu.VMEM((256, 512), F32),
            pltpu.VMEM((128, 512), F32),
            pltpu.VMEM((256, 512), jnp.int32),
            pltpu.VMEM((256, 4), F32),
            dma((3,)),
            dma, dma, dma,
            dma, dma((8,)),
            dma, dma((4,)),
            dma, dma((4, 2, 2)),
            dma, dma((8, 2)),
            dma, dma, dma,
            dma, dma((4,)),
            dma, dma,
            dma, dma,
            dma, dma,
        ],
        compiler_params=pltpu.CompilerParams(
            collective_id=0, has_side_effects=True, vmem_limit_bytes=48 << 20
        ),
        cost_estimate=pl.CostEstimate(
            flops=6 * 128 * 8192 * 512, bytes_accessed=24 << 20, transcendentals=0
        ),
    )(tokens, cotangent, base_copy, codes, scales)


def solution(mesh):
    return jax.shard_map(
        body,
        mesh=mesh,
        in_specs=(
            P(("replica", "shard"), None),
            P(("replica", "shard"), None),
            P(),
            P("shard", None),
            P("shard", None),
        ),
        out_specs=(P(("replica", "shard"), None), P(("replica", "shard"), None), P("shard", None)),
        check_vma=False,
    )
```

time: 330 us -> 73.3 us (0.22); the launches traced: 325 us -> 73.1 us
  waiting for transfers between devices: 275 us -> 0 us
  Pallas kernels: 0 us -> 65.4 us
  matrix products: 26.6 us -> 0 us
  between operations: 13.8 us -> 0.66 us
    reduce_scatter x1 -> x0, waiting for transfers between devices: 134 us -> none  [body(): lax.psum_scatter(lax.dot_general(columns, cotangent, (((0,), (0,)), ((),...]
    psum x1 -> x0, waiting for transfers between devices: 72.6 us -> none  [body(): weight_grad = lax.psum(shard_sum, 'replica')]
    all_gather x1 -> x0, waiting for transfers between devices: 67.5 us -> none  [body(): lax.all_gather(difference, 'shard', axis=0, tiled=True).astype(jnp.float32)]
    pallas_call x0 -> x1, Pallas kernels: none -> 65.4 us  [body(): pl.pallas_call(kernel, out_shape=(jax.ShapeDtypeStruct((128, 512), BF16),...]
    dot_general x3 -> x0, matrix products: 26.6 us -> none  [the longest x1 9.48 us: body(): lax.dot_general(cotangent, weight, (((1,), (1,)), ((), ())), preferred_el...]
    unnamed x8 -> x10, local copies, waits for them, and re-layouts: 7.67 us -> 7.12 us
  transfers between devices with their start and end apart: 3 -> 0, of which waited for: 3 -> 0; matrix products, arithmetic and copies ran while one was open for 10% -> 0% of each run, Pallas kernels for 0% -> 0%
where the time goes in v1:
time: 73.3 us; the launch traced here: 73.1 us
  Pallas kernels  65.4 us (89%)
  local copies, waits for them, and re-layouts  7.12 us (10%)
    pallas_call x1, Pallas kernels, body(): pl.pallas_call(kernel, out_shape=(jax.ShapeDtypeStruct((128, 512), BF16),...  65.4 us
    unnamed x10, local copies, waits for them, and re-layouts  7.12 us

profile of v1, /device:TPU:1, one launch (start us, length us, event | category | flops | bytes accessed | tf_op | source)
XLA Modules:
  0.0 73.1 jit_solution(10476103670039480400)
XLA Ops:
  0.6 0.8 %copy.8.scales = f32[256,4]{1,0:T(8,128)S(1)} copy(f32[256,4]{0,1:T(4,128)} %param.9) | data formatting | bytes 8192 | tf_op args[4]
  1.5 0.0 copy-start
  1.5 1.6 %copy-done = bf16[128,8192]{1,0:T(8,128)(2,1)S(1)} copy-done((bf16[128,8192]{1,0:T(8,128)(2,1)S(1)}, bf16[128,8192]{1,0:T(8,128)(2,1)}, u32[]{:S(2)}) %copy-start) | copy-done | bytes 2097176
  3.0 0.0 copy-start.1
  3.1 1.0 %copy-done.1 = s32[256,512]{1,0:T(8,128)S(1)} copy-done((s32[256,512]{1,0:T(8,128)S(1)}, s32[256,512]{1,0:T(8,128)}, u32[]{:S(2)}) %copy-start.1) | copy-done | bytes 524312
  4.1 0.0 copy-start.2
  4.1 0.9 %copy-done.2 = bf16[128,512]{1,0:T(8,128)(2,1)S(1)} copy-done((bf16[128,512]{1,0:T(8,128)(2,1)S(1)}, bf16[128,512]{1,0:T(8,128)(2,1)}, u32[]{:S(2)}) %copy-start.2) | copy-done | bytes 131096
  5.0 65.4 %shard_map.76 = (bf16[128,512]{1,0:T(8,128)(2,1)S(1)}, bf16[128,8192]{1,0:T(8,128)(2,1)S(1)}, f32[256,512]{1,0:T(8,128)S(1)}) custom-call(bf16[128,8192]{1,0:T(8,128)(2,1)S(1)} %copy-done, bf16[128,512]{1,0:T(8,128)(2,1)S(1)} %copy-done.2, bf16[8192,512]{1,0:T(8,128)(2,1)} %base.1, s32[256,512]{1,0:T(8,128)S(1)} %copy-done.1, f32[256,4]{1,0:T(8,128)S(1)} %copy.8.scales), custom_call_target="tpu_custom_call" | custom-call | flops 3221225472 | bytes 25165824 | tf_op jit(solution)/shard_map/pallas_call | solution.py:313
  70.4 0.7 copy.12
  71.0 1.3 %copy.13 = bf16[128,8192]{1,0:T(8,128)(2,1)} copy(bf16[128,8192]{1,0:T(8,128)(2,1)S(1)} %get-tuple-element.7) | data formatting | bytes 4194304
  72.3 0.8 %copy.14 = f32[256,512]{1,0:T(8,128)} copy(f32[256,512]{1,0:T(8,128)S(1)} %get-tuple-element.8) | data formatting | bytes 1048576
Async XLA Ops:
  1.5 1.6 %copy-start = (bf16[128,8192]{1,0:T(8,128)(2,1)S(1)}, bf16[128,8192]{1,0:T(8,128)(2,1)}, u32[]{:S(2)}) copy-start(bf16[128,8192]{1,0:T(8,128)(2,1)} %tok.1) | copy-start | bytes 6291460
  3.0 1.0 %copy-start.1 = (s32[256,512]{1,0:T(8,128)S(1)}, s32[256,512]{1,0:T(8,128)}, u32[]{:S(2)}) copy-start(s32[256,512]{1,0:T(8,128)} %codes.1) | copy-start | bytes 1572868
  4.1 0.9 %copy-start.2 = (bf16[128,512]{1,0:T(8,128)(2,1)S(1)}, bf16[128,512]{1,0:T(8,128)(2,1)}, u32[]{:S(2)}) copy-start(bf16[128,512]{1,0:T(8,128)(2,1)} %cot.1) | copy-start | bytes 393220

commit v2 on v1

--- a/solution.py
+++ b/solution.py
@@ -15,7 +15,7 @@
     tok, cot, base, codes, scales,
     proj, igrad, wgrad,
     W, BASE, TK, CA, TW, GF, GX, XR, ZS, ZR, RB, RR, IG, PA, PR, CO, SC,
-    ld, tk_l, tk_s, tk_r, ca_s, ca_r, tw_s, tw_r, az_s, az_r, ax_s, ax_r,
+    ld, tk_l, tk_s, tk_r, ca_s, ca_r, tw_s, tw_r, az_s, az_r, bz_s, bz_r, ao_s, ax_s, ax_r,
     ig_l, ig_s, ig_r, gx_s, gx_r, zs_s, zs_r, rr_s, rr_r, pa_s, pa_r,
 ):
     r = lax.axis_index("replica")
@@ -68,9 +68,10 @@
     wait(CO, ld.at[0])
     wait(SC, ld.at[1])
     own = l * 8 + z
+    by_row = SC[...].T
     for g in range(4):
         lanes = pl.ds(g * 128, 128)
-        W[own, :, lanes] = (CO[:, lanes].astype(F32) * SC[:, g : g + 1]).astype(BF16)
+        W[own, :, lanes] = (CO[:, lanes].astype(F32) * by_row[:, g : g + 1]).astype(BF16)
 
     pl.semaphore_wait(barrier, len(peers))
 
@@ -80,17 +81,21 @@
     def send_z(block, t, way, h):
         send(half(block, h), half(block, h), az_s, az_r.at[t, way, h], (up, down)[way])
 
+    def few(block, h):
+        return W.at[block, pl.ds(h * 128, 32)]
+
+    def most(block, h):
+        return W.at[block, pl.ds(h * 128 + 32, 96)]
+
+    def send_few(block, t, way, h):
+        send(few(block, h), few(block, h), bz_s, bz_r.at[t, way, h], (up, down)[way])
+
     def send_x(block, zz, h):
-        send(half(block, h), half(block, h), ax_s, ax_r.at[zz, h], (A, B)[h])
-
-    for h in range(2):
-        send_z(own, 0, 0, h)
-        send_z(own, 0, 1, h)
-        send_x(own, z, h)
-
-    send(cot, CA.at[me8], ca_s, ca_r.at[me8], peer)
+        send(most(block, h), most(block, h), ax_s, ax_r.at[zz, h], (A, B)[h])
+
     for d in (1, 3, 2):
         send(cot, CA.at[me8], ca_s, ca_r.at[me8], dev(y=(y + d) % 4))
+    send(cot, CA.at[me8], ca_s, ca_r.at[me8], peer)
 
     def send_tokens(b, _):
         src = pl.ds(col(b, oc), 256)
@@ -98,8 +103,6 @@
         send(tok.at[:, src], TK.at[pl.ds(c * 128, 128), dst], tk_s, tk_r, peer)
         return 0
 
-    lax.fori_loop(0, 16, send_tokens, 0)
-
     my_rows = pl.ds(pl.multiple_of(me8 * 128, 128), 128)
 
     def kof(i):
@@ -110,24 +113,26 @@
             ((p * 8 + 2 * kof(i) + j % 2) * 2 + core) * 256 + (j // 2) * 128, 128
         )
 
-    def send_part(i):
-        for p in range(2):
-            dst = TW.at[i, my_rows, pl.ds(p * 128, 128)]
-            pltpu.make_async_copy(
-                tok.at[:, pl.ds(chunk(p, i, y, c), 128)], dst, tw_r.at[i]
-            ).start()
+    def send_parts(i):
+        for e, p in ((0, 1 - l), (1, l)):
+            n = 2 * i + e
+            dst = TW.at[n, my_rows]
             for d in (1, 3, 2, 0):
                 j = (y + d) % 4
                 for cc in (c, oc):
+                    src = tok.at[:, pl.ds(chunk(p, i, j, cc), 128)]
                     if d == 0 and cc is c:
-                        continue
-                    send(
-                        tok.at[:, pl.ds(chunk(p, i, j, cc), 128)], dst, tw_s, tw_r.at[i],
-                        dev(y=j, c=cc),
-                    )
-
-    send_part(0)
-    send_part(1)
+                        pltpu.make_async_copy(src, dst, tw_r.at[n]).start()
+                    else:
+                        send(src, dst, tw_s, tw_r.at[n], dev(y=j, c=cc))
+
+    send_parts(0)
+    for h in range(2):
+        send(half(own, h), half(own, h), ao_s, ax_r.at[z, h], (A, B)[h])
+        send_z(own, 0, 0, h)
+        send_z(own, 0, 1, h)
+    lax.fori_loop(0, 16, send_tokens, 0)
+    send_parts(1)
 
     PA[...] = jnp.zeros_like(PA)
     wait(CA.at[me8], ca_r.at[me8])
@@ -144,10 +149,10 @@
         zz = lax.rem(z + offset(m), 8)
         block = jnp.where(other, (1 - l) * 8 + zz, l * 8 + zz)
 
-        @pl.when(other)
+        @pl.when(jnp.logical_and(other, m > 0))
         def _():
             for h in range(2):
-                wait(half(block, h), ax_r.at[zz, h])
+                wait(most(block, h), ax_r.at[zz, h])
 
         w = (BASE[block].astype(F32) + W[block].astype(F32)).astype(BF16)
         lanes = pl.ds(pl.multiple_of(block * 256, 256), 256)
@@ -162,12 +167,12 @@
         send(theirs, out, ig_s, ig_r, peer)
         pltpu.make_async_copy(mine, out, ig_l).start()
 
-    def piece(p, half_x):
-        return pl.multiple_of(p * 128 + half_x * 64, 64)
+    def x_rows(half_x):
+        return pl.ds(pl.multiple_of(half_x * 64, 64), 64)
 
     def x_sum(i):
         wait(XR.at[i], gx_r.at[i])
-        total = GF[pl.ds(piece(l, X), 64), :]
+        total = GF[i % 2, x_rows(X), :]
         for q in range(3):
             total = total + XR[i, q].astype(F32)
         ZS[i] = total.astype(BF16)
@@ -181,7 +186,14 @@
         def _():
             ZR[z] = total.astype(BF16)
 
-    def part(i):
+    def product(n):
+        wait(TW.at[n], tw_r.at[n])
+        return lax.dot_general(
+            TW[n], CA[...].reshape(1024, 512), (((0,), (0,)), ((), ())),
+            preferred_element_type=F32,
+        )
+
+    def parts(i):
         @pl.when(i == 0)
         def _():
             for d in (1, 3, 2):
@@ -192,19 +204,27 @@
                 k = ((y + d) % 4) * 2 + oc
                 wait(CA.at[k], ca_r.at[k])
 
-        wait(TW.at[i], tw_r.at[i])
-        GF[...] = lax.dot_general(
-            TW[i], CA[...].reshape(1024, 512), (((0,), (0,)), ((), ())),
-            preferred_element_type=F32,
-        )
-        GX[i] = GF[...].astype(BF16)
-        for q, (p, hx, to) in enumerate(((1 - l, X, A), (1 - l, 1 - X, B), (l, 1 - X, O))):
-            send(GX.at[i, pl.ds(piece(p, hx), 64)], XR.at[i, q], gx_s, gx_r.at[i], to)
+        GX[2 * i] = product(2 * i).astype(BF16)
+        send(GX.at[2 * i, x_rows(X)], XR.at[i, 0], gx_s, gx_r.at[i], A)
+        send(GX.at[2 * i, x_rows(1 - X)], XR.at[i, 1], gx_s, gx_r.at[i], B)
+        GF[i % 2] = product(2 * i + 1)
+        GX[2 * i + 1] = GF[i % 2].astype(BF16)
+        send(GX.at[2 * i + 1, x_rows(1 - X)], XR.at[i, 2], gx_s, gx_r.at[i], O)
+
+    beside = (1 - l) * 8 + z
 
     def step(i, _):
         @pl.when(i < 4)
         def _():
             t = i
+
+            @pl.when(t == 0)
+            def _():
+                for h in range(2):
+                    wait(half(beside, h), ax_r.at[z, h])
+                    send_few(beside, 0, 0, h)
+                    send_few(beside, 0, 1, h)
+
             zu, zd = lax.rem(z + 7 - t, 8), lax.rem(z + t + 1, 8)
             for h in range(2):
                 for way, zz in ((0, zu), (1, zd)):
@@ -220,9 +240,21 @@
 
                         send_x(block, zz, h)
 
+            for h in range(2):
+                for way, zz in ((0, zu), (1, zd)):
+                    block2 = (1 - l) * 8 + zz
+
+                    @pl.when(jnp.logical_or(t < 3, h == way))
+                    def _():
+                        wait(few(block2, h), bz_r.at[t, way, h])
+
+                        @pl.when(jnp.logical_or(t < 2, jnp.logical_and(t == 2, h == way)))
+                        def _():
+                            send_few(block2, t + 1, way, h)
+
         @pl.when(i < 2)
         def _():
-            send_part(i + 2)
+            send_parts(i + 2)
 
         lo1 = jnp.where(i == 0, 0, jnp.minimum(2 * i + 1, 8))
         hi1 = jnp.minimum(2 * i + 3, 8)
@@ -247,7 +279,7 @@
 
         @pl.when(i < 4)
         def _():
-            part(i)
+            parts(i)
 
         return 0
 
@@ -289,7 +321,9 @@
     wait(CA.at[pl.ds(0, 7)], ca_s)
     wait(TW.at[:, pl.ds(0, 896)], tw_s)
     wait(W.at[pl.ds(0, 7)], az_s)
-    wait(W.at[pl.ds(0, 8)], ax_s)
+    wait(W.at[pl.ds(0, 7), pl.ds(0, 64)], bz_s)
+    wait(W.at[0], ao_s)
+    wait(W.at[pl.ds(0, 7), pl.ds(0, 192)], ax_s)
     wait(XR, gx_s)
     wait(PR, pa_s)
 
@@ -307,16 +341,38 @@
     wait(half_tokens, ig_r)
 
 
+def finish(p_in, i_in, w_in, p_out, i_out, w_out, p_buf, i_buf, w_buf, sem_in, sem_out):
+    pieces = [(w_in, w_buf, w_out)]
+    pieces += [
+        tuple(ref.at[pl.ds(n * 32, 32)] for ref in (i_in, i_buf, i_out)) for n in range(4)
+    ]
+    pieces += [(p_in, p_buf, p_out)]
+    loads = [
+        pltpu.make_async_copy(src, buf, sem_in.at[n]) for n, (src, buf, _) in enumerate(pieces)
+    ]
+    stores = [
+        pltpu.make_async_copy(buf, dst, sem_out.at[n]) for n, (_, buf, dst) in enumerate(pieces)
+    ]
+    for load in loads:
+        load.start()
+    for load, store in zip(loads, stores):
+        load.wait()
+        store.start()
+    for store in stores:
+        store.wait()
+
+
 def body(tokens, cotangent, base_copy, codes, scales):
     dma = pltpu.SemaphoreType.DMA
     anywhere = pl.BlockSpec(memory_space=pl.ANY)
-    return pl.pallas_call(
+    shapes = (
+        jax.ShapeDtypeStruct((128, 512), BF16),
+        jax.ShapeDtypeStruct((128, 8192), BF16),
+        jax.ShapeDtypeStruct((256, 512), F32),
+    )
+    results = pl.pallas_call(
         kernel,
-        out_shape=(
-            jax.ShapeDtypeStruct((128, 512), BF16),
-            jax.ShapeDtypeStruct((128, 8192), BF16),
-            jax.ShapeDtypeStruct((256, 512), F32),
-        ),
+        out_shape=shapes,
         in_specs=[anywhere] * 5,
         out_specs=(
             pl.BlockSpec(memory_space=pltpu.VMEM),
@@ -328,9 +384,9 @@
             pltpu.VMEM((16, 256, 512), BF16),
             pltpu.VMEM((256, 4096), BF16),
             pltpu.VMEM((8, 128, 512), BF16),
-            pltpu.VMEM((4, 1024, 256), BF16),
-            pltpu.VMEM((256, 512), F32),
-            pltpu.VMEM((4, 256, 512), BF16),
+            pltpu.VMEM((8, 1024, 128), BF16),
+            pltpu.VMEM((2, 128, 512), F32),
+            pltpu.VMEM((8, 128, 512), BF16),
             pltpu.VMEM((4, 3, 64, 512), BF16),
             pltpu.VMEM((4, 64, 512), BF16),
             pltpu.VMEM((8, 64, 512), BF16),
@@ -340,12 +396,14 @@
             pltpu.VMEM((256, 512), F32),
             pltpu.VMEM((128, 512), F32),
             pltpu.VMEM((256, 512), jnp.int32),
-            pltpu.VMEM((256, 4), F32),
+            pltpu.VMEM((4, 256), F32),
             dma((3,)),
             dma, dma, dma,
             dma, dma((8,)),
-            dma, dma((4,)),
+            dma, dma((8,)),
             dma, dma((4, 2, 2)),
+            dma, dma((4, 2, 2)),
+            dma,
             dma, dma((8, 2)),
             dma, dma, dma,
             dma, dma((4,)),
@@ -354,12 +412,26 @@
             dma, dma,
         ],
         compiler_params=pltpu.CompilerParams(
-            collective_id=0, has_side_effects=True, vmem_limit_bytes=48 << 20
+            collective_id=0, has_side_effects=True, vmem_limit_bytes=62 << 20
         ),
         cost_estimate=pl.CostEstimate(
             flops=6 * 128 * 8192 * 512, bytes_accessed=24 << 20, transcendentals=0
         ),
-    )(tokens, cotangent, base_copy, codes, scales)
+    )(tokens, cotangent, base_copy, codes, scales.T)
+    return pl.pallas_call(
+        finish,
+        out_shape=shapes,
+        in_specs=[anywhere] * 3,
+        out_specs=(anywhere,) * 3,
+        scratch_shapes=[
+            pltpu.VMEM((128, 512), BF16),
+            pltpu.VMEM((128, 8192), BF16),
+            pltpu.VMEM((256, 512), F32),
+            dma((6,)),
+            dma((6,)),
+        ],
+        compiler_params=pltpu.CompilerParams(vmem_limit_bytes=62 << 20),
+    )(*results)
 
 
 def solution(mesh):

time: 73.3 us -> 65.4 us (0.89)
  local copies, waits for them, and re-layouts: 7.12 us -> 0 us
  Pallas kernels: 65.4 us -> 64.6 us
    unnamed x10 -> x0, local copies, waits for them, and re-layouts: 7.12 us -> none
    pallas_call x1 -> x2, Pallas kernels: 65.4 us -> 64.6 us  [the longest x1 62 us: body(): pl.pallas_call(kernel, out_shape=shapes, in_specs=[anywhere] * 5, out_spe...]
where the time goes in v2:
time: 65.4 us; the launch traced here: 65.3 us
  Pallas kernels  64.6 us (99%)
    pallas_call x1, Pallas kernels, body(): pl.pallas_call(kernel, out_shape=shapes, in_specs=[anywhere] * 5, out_spe...  62 us
    pallas_call x1, Pallas kernels, body(): pl.pallas_call(finish, out_shape=shapes, in_specs=[anywhere] * 3, out_spe...  2.66 us

profile of v2, /device:TPU:1, one launch (start us, length us, event | category | flops | bytes accessed | tf_op | source)
XLA Modules:
  0.0 65.3 jit_solution(17941025916840814684)
XLA Ops:
  0.6 62.0 %shard_map.76 = (bf16[128,512]{1,0:T(8,128)(2,1)}, bf16[128,8192]{1,0:T(8,128)(2,1)}, f32[256,512]{1,0:T(8,128)}) custom-call(bf16[128,8192]{1,0:T(8,128)(2,1)} %tok.1, bf16[128,512]{1,0:T(8,128)(2,1)} %cot.1, bf16[8192,512]{1,0:T(8,128)(2,1)} %base.1, s32[256,512]{1,0:T(8,128)} %codes.1, f32[4,256]{1,0:T(4,128)} %bitcast.1), custom_call_target="tpu_custom_call" | custom-call | flops 3221225472 | bytes 25165824 | tf_op jit(solution)/shard_map/pallas_call | solution.py:373
  62.6 2.7 %shard_map.77 = (bf16[128,512]{1,0:T(8,128)(2,1)}, bf16[128,8192]{1,0:T(8,128)(2,1)}, f32[256,512]{1,0:T(8,128)}) custom-call(bf16[128,512]{1,0:T(8,128)(2,1)} %get-tuple-element.6.p_in, bf16[128,8192]{1,0:T(8,128)(2,1)} %get-tuple-element.7.i_in, f32[256,512]{1,0:T(8,128)} %get-tuple-element.8.w_in), custom_call_target="tpu_custom_call" | custom-call | tf_op jit(solution)/shard_map/pallas_call | solution.py:421

commit v3 on v2

--- a/solution.py
+++ b/solution.py
@@ -14,7 +14,7 @@
 def kernel(
     tok, cot, base, codes, scales,
     proj, igrad, wgrad,
-    W, BASE, TK, CA, TW, GF, GX, XR, ZS, ZR, RB, RR, IG, PA, PR, CO, SC,
+    W, BASE, TOK, TT, TK, CA, TW, GF, GX, XR, ZS, ZR, RR, IG, PA, PR, CO, SC,
     ld, tk_l, tk_s, tk_r, ca_s, ca_r, tw_s, tw_r, az_s, az_r, bz_s, bz_r, ao_s, ax_s, ax_r,
     ig_l, ig_s, ig_r, gx_s, gx_r, zs_s, zs_r, rr_s, rr_r, pa_s, pa_r,
 ):
@@ -37,6 +37,7 @@
     def send(src, dst, ssem, rsem, to):
         pltpu.make_async_remote_copy(src, dst, ssem, rsem, device_id=to).start()
 
+    pltpu.make_async_copy(tok, TOK, ld.at[3]).start()
     pltpu.make_async_copy(codes, CO, ld.at[0]).start()
     pltpu.make_async_copy(scales, SC, ld.at[1]).start()
     me8 = y * 2 + c
@@ -73,6 +74,22 @@
         lanes = pl.ds(g * 128, 128)
         W[own, :, lanes] = (CO[:, lanes].astype(F32) * by_row[:, g : g + 1]).astype(BF16)
 
+    def zof(n):
+        return lax.rem(z + jnp.where(n % 2 == 1, (7 - n) // 2, 4 + n // 2), 8)
+
+    def turn(n):
+        def one(q, _):
+            p, cc = q // 2, q % 2
+            lanes = pl.ds(col(p * 8 + zof(n), cc), 256)
+            TT[n, cc, p] = TOK[:, lanes].T
+            return 0
+
+        lax.fori_loop(0, 4, one, 0)
+
+    wait(TOK, ld.at[3])
+    turn(0)
+    turn(1)
+
     pl.semaphore_wait(barrier, len(peers))
 
     def half(block, h):
@@ -103,36 +120,30 @@
         send(tok.at[:, src], TK.at[pl.ds(c * 128, 128), dst], tk_s, tk_r, peer)
         return 0
 
-    my_rows = pl.ds(pl.multiple_of(me8 * 128, 128), 128)
-
-    def kof(i):
-        return lax.rem(z // 2 + i + 1, 4)
-
-    def chunk(p, i, j, core):
-        return pl.multiple_of(
-            ((p * 8 + 2 * kof(i) + j % 2) * 2 + core) * 256 + (j // 2) * 128, 128
-        )
-
-    def send_parts(i):
-        for e, p in ((0, 1 - l), (1, l)):
-            n = 2 * i + e
-            dst = TW.at[n, my_rows]
-            for d in (1, 3, 2, 0):
-                j = (y + d) % 4
-                for cc in (c, oc):
-                    src = tok.at[:, pl.ds(chunk(p, i, j, cc), 128)]
-                    if d == 0 and cc is c:
-                        pltpu.make_async_copy(src, dst, tw_r.at[n]).start()
-                    else:
-                        send(src, dst, tw_s, tw_r.at[n], dev(y=j, c=cc))
-
-    send_parts(0)
+    my_lanes = pl.ds(pl.multiple_of(me8 * 128, 128), 128)
+
+    def send_part(n):
+        dst = TW.at[n, :, :, my_lanes]
+        for d in (1, 3, 2, 0):
+            j = (y + d) % 4
+            rows = pl.ds(pl.multiple_of(j * 64, 64), 64)
+            for cc in (c, oc):
+                src = TT.at[n, cc, :, rows]
+                if d == 0 and cc is c:
+                    pltpu.make_async_copy(src, dst, tw_r.at[n]).start()
+                else:
+                    send(src, dst, tw_s, tw_r.at[n], dev(y=j, c=cc))
+
+    send_part(0)
     for h in range(2):
         send(half(own, h), half(own, h), ao_s, ax_r.at[z, h], (A, B)[h])
         send_z(own, 0, 0, h)
         send_z(own, 0, 1, h)
     lax.fori_loop(0, 16, send_tokens, 0)
-    send_parts(1)
+    send_part(1)
+    for n in (2, 3):
+        turn(n)
+        send_part(n)
 
     PA[...] = jnp.zeros_like(PA)
     wait(CA.at[me8], ca_r.at[me8])
@@ -167,34 +178,11 @@
         send(theirs, out, ig_s, ig_r, peer)
         pltpu.make_async_copy(mine, out, ig_l).start()
 
-    def x_rows(half_x):
-        return pl.ds(pl.multiple_of(half_x * 64, 64), 64)
-
-    def x_sum(i):
-        wait(XR.at[i], gx_r.at[i])
-        total = GF[i % 2, x_rows(X), :]
-        for q in range(3):
-            total = total + XR[i, q].astype(F32)
-        ZS[i] = total.astype(BF16)
-        to = 2 * kof(i) + y % 2
-
-        @pl.when(to != z)
-        def _():
-            send(ZS.at[i], ZR.at[z], zs_s, zs_r, dev(z=to))
-
-        @pl.when(to == z)
-        def _():
-            ZR[z] = total.astype(BF16)
-
-    def product(n):
-        wait(TW.at[n], tw_r.at[n])
-        return lax.dot_general(
-            TW[n], CA[...].reshape(1024, 512), (((0,), (0,)), ((), ())),
-            preferred_element_type=F32,
-        )
-
-    def parts(i):
-        @pl.when(i == 0)
+    def x_rows(p, half_x):
+        return pl.ds(pl.multiple_of(p * 64 + half_x * 32, 32), 32)
+
+    def part(n):
+        @pl.when(n == 0)
         def _():
             for d in (1, 3, 2):
                 k = ((y + d) % 4) * 2 + c
@@ -204,122 +192,125 @@
                 k = ((y + d) % 4) * 2 + oc
                 wait(CA.at[k], ca_r.at[k])
 
-        GX[2 * i] = product(2 * i).astype(BF16)
-        send(GX.at[2 * i, x_rows(X)], XR.at[i, 0], gx_s, gx_r.at[i], A)
-        send(GX.at[2 * i, x_rows(1 - X)], XR.at[i, 1], gx_s, gx_r.at[i], B)
-        GF[i % 2] = product(2 * i + 1)
-        GX[2 * i + 1] = GF[i % 2].astype(BF16)
-        send(GX.at[2 * i + 1, x_rows(1 - X)], XR.at[i, 2], gx_s, gx_r.at[i], O)
+        wait(TW.at[n], tw_r.at[n])
+        GF[n % 4] = jnp.dot(
+            TW[n].reshape(128, 1024), CA[...].reshape(1024, 512), preferred_element_type=F32
+        )
+        GX[n] = GF[n % 4].astype(BF16)
+        send(GX.at[n, x_rows(l, 1 - X)], XR.at[n, 2], gx_s, gx_r.at[n], O)
+        send(GX.at[n, x_rows(1 - l, X)], XR.at[n, 0], gx_s, gx_r.at[n], A)
+        send(GX.at[n, x_rows(1 - l, 1 - X)], XR.at[n, 1], gx_s, gx_r.at[n], B)
+
+    def x_sum(n):
+        wait(XR.at[n], gx_r.at[n])
+        total = GF[n % 4, x_rows(l, X), :]
+        for q in range(3):
+            total = total + XR[n, q].astype(F32)
+        return total
+
+    def x_stage(n):
+        ZS[n] = x_sum(n).astype(BF16)
+        send(ZS.at[n], ZR.at[z], zs_s, zs_r, dev(z=zof(n)))
 
     beside = (1 - l) * 8 + z
 
     def step(i, _):
-        @pl.when(i < 4)
+        t = i
+
+        @pl.when(t == 0)
         def _():
-            t = i
-
-            @pl.when(t == 0)
-            def _():
-                for h in range(2):
-                    wait(half(beside, h), ax_r.at[z, h])
-                    send_few(beside, 0, 0, h)
-                    send_few(beside, 0, 1, h)
-
-            zu, zd = lax.rem(z + 7 - t, 8), lax.rem(z + t + 1, 8)
             for h in range(2):
-                for way, zz in ((0, zu), (1, zd)):
-                    block = l * 8 + zz
-
-                    @pl.when(jnp.logical_or(t < 3, h == way))
+                wait(half(beside, h), ax_r.at[z, h])
+                send_few(beside, 0, 0, h)
+                send_few(beside, 0, 1, h)
+
+        zu, zd = lax.rem(z + 7 - t, 8), lax.rem(z + t + 1, 8)
+        for h in range(2):
+            for way, zz in ((0, zu), (1, zd)):
+                block = l * 8 + zz
+
+                @pl.when(jnp.logical_or(t < 3, h == way))
+                def _():
+                    wait(half(block, h), az_r.at[t, way, h])
+
+                    @pl.when(jnp.logical_or(t < 2, jnp.logical_and(t == 2, h == way)))
                     def _():
-                        wait(half(block, h), az_r.at[t, way, h])
-
-                        @pl.when(jnp.logical_or(t < 2, jnp.logical_and(t == 2, h == way)))
-                        def _():
-                            send_z(block, t + 1, way, h)
-
-                        send_x(block, zz, h)
-
-            for h in range(2):
-                for way, zz in ((0, zu), (1, zd)):
-                    block2 = (1 - l) * 8 + zz
-
-                    @pl.when(jnp.logical_or(t < 3, h == way))
+                        send_z(block, t + 1, way, h)
+
+                    send_x(block, zz, h)
+
+        for h in range(2):
+            for way, zz in ((0, zu), (1, zd)):
+                block2 = (1 - l) * 8 + zz
+
+                @pl.when(jnp.logical_or(t < 3, h == way))
+                def _():
+                    wait(few(block2, h), bz_r.at[t, way, h])
+
+                    @pl.when(jnp.logical_or(t < 2, jnp.logical_and(t == 2, h == way)))
                     def _():
-                        wait(few(block2, h), bz_r.at[t, way, h])
-
-                        @pl.when(jnp.logical_or(t < 2, jnp.logical_and(t == 2, h == way)))
-                        def _():
-                            send_few(block2, t + 1, way, h)
+                        send_few(block2, t + 1, way, h)
 
         @pl.when(i < 2)
         def _():
-            send_parts(i + 2)
-
-        lo1 = jnp.where(i == 0, 0, jnp.minimum(2 * i + 1, 8))
-        hi1 = jnp.minimum(2 * i + 3, 8)
-        lo2 = jnp.maximum(2 * i - 1, 0)
-        hi2 = jnp.minimum(2 * i + 1, 8)
-        n1 = hi1 - lo1
+            for e in range(2):
+                turn(2 * i + 4 + e)
+                send_part(2 * i + 4 + e)
+
+        lo1 = jnp.where(i == 0, 0, 2 * i + 1)
+        n1 = jnp.minimum(2 * i + 3, 8) - lo1
+        lo2 = jnp.maximum(2 * i - 3, 0)
+        n2 = jnp.maximum(2 * i - 1, 0) - lo2
 
         def one(n, _):
             other = n >= n1
             use_block(other, jnp.where(other, lo2 + n - n1, lo1 + n))
             return 0
 
-        lax.fori_loop(0, n1 + hi2 - lo2, one, 0)
-
-        @pl.when(i == 4)
-        def _():
-            send(PA.at[pl.ds(pl.multiple_of(oc * 128, 128), 128)], PR, pa_s, pa_r, peer)
-
-        @pl.when(i > 0)
-        def _():
-            x_sum(i - 1)
-
-        @pl.when(i < 4)
-        def _():
-            parts(i)
+        lax.fori_loop(0, n1 + n2, one, 0)
+
+        for n in (2 * i, 2 * i + 1):
+
+            @pl.when(i > 0)
+            def _():
+                x_stage(n - 2)
+
+            part(n)
 
         return 0
 
-    lax.fori_loop(0, 5, step, 0)
-
-    holds = z % 2 == y % 2
-    slot = (y // 2) * 2 + X
-
-    @pl.when(holds)
-    def _():
-        wait(ZR.at[pl.ds(0, 7)], zs_r)
-        total = ZR[0].astype(F32)
-        for q in range(1, 8):
-            total = total + ZR[q].astype(F32)
-        total = (total * (1.0 / math.sqrt(32768.0))).astype(BF16)
-        RB[...] = total
-        for XX in (X, 1 - X):
-            for d in (1, 2, 3, 0):
-                if XX is X and d == 0:
-                    continue
-                send(RB, RR.at[slot], rr_s, rr_r, dev(X=XX, y=(y + d) % 4))
-        RR[slot] = total
+    lax.fori_loop(0, 4, step, 0)
+
+    x_stage(6)
+    total = x_sum(7)
+    wait(ZR.at[pl.ds(0, 7)], zs_r)
+    for d in range(1, 8):
+        total = total + ZR[lax.rem(z + d, 8)].astype(F32)
+    my_piece = pl.ds(pl.multiple_of((y * 2 + X) * 32, 32), 32)
+    RR[my_piece, :] = (total * (1.0 / math.sqrt(32768.0))).astype(BF16)
+    for XX in (1 - X, X):
+        for d in (2, 1, 3, 0):
+            if XX is X and d == 0:
+                continue
+            to = dev(X=XX, y=(y + d) % 4)
+            send(RR.at[my_piece], RR.at[my_piece], rr_s, rr_r, to)
+
+    def last(m, _):
+        use_block(True, m)
+        return 0
+
+    lax.fori_loop(5, 8, last, 0)
+    send(PA.at[pl.ds(pl.multiple_of(oc * 128, 128), 128)], PR, pa_s, pa_r, peer)
 
     wait(PR, pa_r)
     proj[...] = (PA[pl.ds(pl.multiple_of(c * 128, 128), 128), :] + PR[...]).astype(BF16)
 
-    @pl.when(holds)
-    def _():
-        wait(RR.at[pl.ds(0, 3)], rr_r)
-
-    @pl.when(jnp.logical_not(holds))
-    def _():
-        wait(RR, rr_r)
-
-    for q in range(4):
-        wgrad[pl.ds(q * 64, 64), :] = RR[q].astype(F32)
+    wait(RR.at[pl.ds(0, 224)], rr_r)
+    wgrad[...] = RR[...].astype(F32)
 
     wait(half_tokens, tk_s)
     wait(CA.at[pl.ds(0, 7)], ca_s)
-    wait(TW.at[:, pl.ds(0, 896)], tw_s)
+    wait(TW.at[:, :, :, pl.ds(0, 896)], tw_s)
     wait(W.at[pl.ds(0, 7)], az_s)
     wait(W.at[pl.ds(0, 7), pl.ds(0, 64)], bz_s)
     wait(W.at[0], ao_s)
@@ -327,15 +318,8 @@
     wait(XR, gx_s)
     wait(PR, pa_s)
 
-    @pl.when(holds)
-    def _():
-        wait(ZS.at[pl.ds(0, 3)], zs_s)
-        wait(ZR.at[pl.ds(0, 7)], rr_s)
-
-    @pl.when(jnp.logical_not(holds))
-    def _():
-        wait(ZS, zs_s)
-
+    wait(ZS, zs_s)
+    wait(ZR.at[pl.ds(0, 7)], rr_s)
     wait(half_tokens, ig_s)
     wait(half_tokens, ig_l)
     wait(half_tokens, ig_r)
@@ -382,22 +366,23 @@
         scratch_shapes=[
             pltpu.VMEM((16, 256, 512), BF16),
             pltpu.VMEM((16, 256, 512), BF16),
+            pltpu.VMEM((128, 8192), BF16),
+            pltpu.VMEM((8, 2, 2, 256, 128), BF16),
             pltpu.VMEM((256, 4096), BF16),
             pltpu.VMEM((8, 128, 512), BF16),
-            pltpu.VMEM((8, 1024, 128), BF16),
-            pltpu.VMEM((2, 128, 512), F32),
+            pltpu.VMEM((8, 2, 64, 1024), BF16),
+            pltpu.VMEM((4, 128, 512), F32),
             pltpu.VMEM((8, 128, 512), BF16),
-            pltpu.VMEM((4, 3, 64, 512), BF16),
-            pltpu.VMEM((4, 64, 512), BF16),
-            pltpu.VMEM((8, 64, 512), BF16),
-            pltpu.VMEM((64, 512), BF16),
-            pltpu.VMEM((4, 64, 512), BF16),
+            pltpu.VMEM((8, 3, 32, 512), BF16),
+            pltpu.VMEM((7, 32, 512), BF16),
+            pltpu.VMEM((8, 32, 512), BF16),
+            pltpu.VMEM((256, 512), BF16),
             pltpu.VMEM((16, 256, 256), BF16),
             pltpu.VMEM((256, 512), F32),
             pltpu.VMEM((128, 512), F32),
             pltpu.VMEM((256, 512), jnp.int32),
             pltpu.VMEM((4, 256), F32),
-            dma((3,)),
+            dma((4,)),
             dma, dma, dma,
             dma, dma((8,)),
             dma, dma((8,)),
@@ -406,7 +391,7 @@
             dma,
             dma, dma((8, 2)),
             dma, dma, dma,
-            dma, dma((4,)),
+            dma, dma((8,)),
             dma, dma,
             dma, dma,
             dma, dma,

time: 65.4 us -> 60.5 us (0.925)
  Pallas kernels: 64.6 us -> 59.7 us
    pallas_call x1, Pallas kernels: 62 us -> 57 us  [body(): pl.pallas_call(kernel, out_shape=shapes, in_specs=[anywhere] * 5, out_spe...]
where the time goes in v3:
time: 60.5 us; the launch traced here: 60.3 us
  Pallas kernels  59.7 us (99%)
  between operations  0.64 us (1%)
    pallas_call x1, Pallas kernels, body(): pl.pallas_call(kernel, out_shape=shapes, in_specs=[anywhere] * 5, out_spe...  57 us
    pallas_call x1, Pallas kernels, body(): pl.pallas_call(finish, out_shape=shapes, in_specs=[anywhere] * 3, out_spe...  2.66 us

profile of v3, /device:TPU:1, one launch (start us, length us, event | category | flops | bytes accessed | tf_op | source)
XLA Modules:
  0.0 60.3 jit_solution(731842396866672777)
XLA Ops:
  0.6 57.0 %shard_map.76 = (bf16[128,512]{1,0:T(8,128)(2,1)}, bf16[128,8192]{1,0:T(8,128)(2,1)}, f32[256,512]{1,0:T(8,128)}) custom-call(bf16[128,8192]{1,0:T(8,128)(2,1)} %tok.1, bf16[128,512]{1,0:T(8,128)(2,1)} %cot.1, bf16[8192,512]{1,0:T(8,128)(2,1)} %base.1, s32[256,512]{1,0:T(8,128)} %codes.1, f32[4,256]{1,0:T(4,128)} %bitcast.1), custom_call_target="tpu_custom_call" | custom-call | flops 3221225472 | bytes 25165824 | tf_op jit(solution)/shard_map/pallas_call | solution.py:357
  57.7 2.7 %shard_map.77 = (bf16[128,512]{1,0:T(8,128)(2,1)}, bf16[128,8192]{1,0:T(8,128)(2,1)}, f32[256,512]{1,0:T(8,128)}) custom-call(bf16[128,512]{1,0:T(8,128)(2,1)} %get-tuple-element.6.p_in, bf16[128,8192]{1,0:T(8,128)(2,1)} %get-tuple-element.7.i_in, f32[256,512]{1,0:T(8,128)} %get-tuple-element.8.w_in), custom_call_target="tpu_custom_call" | custom-call | tf_op jit(solution)/shard_map/pallas_call | solution.py:406

commit v4 on v3

--- a/solution.py
+++ b/solution.py
@@ -46,7 +46,7 @@
     barrier = pltpu.get_barrier_semaphore()
     peers = [peer]
     peers += [dev(y=(y + d) % 4, c=cc) for d in (1, 2, 3) for cc in (c, oc)]
-    peers += [dev(z=(z + d) % 8) for d in range(1, 8)]
+    peers += [up, down]
     peers += [A, B, O]
     peers += [dev(X=1 - X, y=(y + d) % 4) for d in (1, 2, 3)]
     for d in peers:
@@ -66,16 +66,8 @@
 
     lax.fori_loop(0, 16, load_block, 0)
 
-    wait(CO, ld.at[0])
-    wait(SC, ld.at[1])
-    own = l * 8 + z
-    by_row = SC[...].T
-    for g in range(4):
-        lanes = pl.ds(g * 128, 128)
-        W[own, :, lanes] = (CO[:, lanes].astype(F32) * by_row[:, g : g + 1]).astype(BF16)
-
     def zof(n):
-        return lax.rem(z + jnp.where(n % 2 == 1, (7 - n) // 2, 4 + n // 2), 8)
+        return lax.rem(z + jnp.where(n % 2 == 1, 8 - (7 - n) // 2, 4 - n // 2), 8)
 
     def turn(n):
         def one(q, _):
@@ -86,10 +78,6 @@
 
         lax.fori_loop(0, 4, one, 0)
 
-    wait(TOK, ld.at[3])
-    turn(0)
-    turn(1)
-
     pl.semaphore_wait(barrier, len(peers))
 
     def half(block, h):
@@ -99,10 +87,10 @@
         send(half(block, h), half(block, h), az_s, az_r.at[t, way, h], (up, down)[way])
 
     def few(block, h):
-        return W.at[block, pl.ds(h * 128, 32)]
+        return W.at[block, pl.ds(h * 128, 48)]
 
     def most(block, h):
-        return W.at[block, pl.ds(h * 128 + 32, 96)]
+        return W.at[block, pl.ds(h * 128 + 48, 80)]
 
     def send_few(block, t, way, h):
         send(few(block, h), few(block, h), bz_s, bz_r.at[t, way, h], (up, down)[way])
@@ -134,16 +122,22 @@
                 else:
                     send(src, dst, tw_s, tw_r.at[n], dev(y=j, c=cc))
 
-    send_part(0)
+    wait(CO, ld.at[0])
+    wait(SC, ld.at[1])
+    own = l * 8 + z
+    by_row = SC[...].T
+    for g in range(4):
+        lanes = pl.ds(g * 128, 128)
+        W[own, :, lanes] = (CO[:, lanes].astype(F32) * by_row[:, g : g + 1]).astype(BF16)
     for h in range(2):
         send(half(own, h), half(own, h), ao_s, ax_r.at[z, h], (A, B)[h])
         send_z(own, 0, 0, h)
         send_z(own, 0, 1, h)
-    lax.fori_loop(0, 16, send_tokens, 0)
-    send_part(1)
-    for n in (2, 3):
+    wait(TOK, ld.at[3])
+    for n in range(4):
         turn(n)
         send_part(n)
+    lax.fori_loop(0, 16, send_tokens, 0)
 
     PA[...] = jnp.zeros_like(PA)
     wait(CA.at[me8], ca_r.at[me8])
@@ -158,12 +152,16 @@
 
     def use_block(other, m):
         zz = lax.rem(z + offset(m), 8)
-        block = jnp.where(other, (1 - l) * 8 + zz, l * 8 + zz)
-
-        @pl.when(jnp.logical_and(other, m > 0))
-        def _():
+        block = jnp.where(other, 1 - l, l) * 8 + zz
+
+        def arrive():
             for h in range(2):
                 wait(most(block, h), ax_r.at[zz, h])
+
+        if other is True:
+            arrive()
+        else:
+            pl.when(jnp.logical_and(other, m > 0))(arrive)
 
         w = (BASE[block].astype(F32) + W[block].astype(F32)).astype(BF16)
         lanes = pl.ds(pl.multiple_of(block * 256, 256), 256)
@@ -208,9 +206,23 @@
             total = total + XR[n, q].astype(F32)
         return total
 
-    def x_stage(n):
-        ZS[n] = x_sum(n).astype(BF16)
-        send(ZS.at[n], ZR.at[z], zs_s, zs_r, dev(z=zof(n)))
+    def x_stage(n, even):
+        total = x_sum(n)
+
+        def pass_on():
+            wait(ZR.at[n - 2], zs_r.at[n - 2])
+            ZS[n] = (total + ZR[n - 2].astype(F32)).astype(BF16)
+
+        if isinstance(n, int):
+            pass_on()
+        else:
+            pl.when(n >= 2)(pass_on)
+
+            @pl.when(n < 2)
+            def _():
+                ZS[n] = total.astype(BF16)
+
+        send(ZS.at[n], ZR.at[n], zs_s, zs_r.at[n], up if even else down)
 
     beside = (1 - l) * 8 + z
 
@@ -269,11 +281,12 @@
 
         lax.fori_loop(0, n1 + n2, one, 0)
 
-        for n in (2 * i, 2 * i + 1):
+        for e in range(2):
+            n = 2 * i + e
 
             @pl.when(i > 0)
             def _():
-                x_stage(n - 2)
+                x_stage(n - 2, e == 0)
 
             part(n)
 
@@ -281,11 +294,13 @@
 
     lax.fori_loop(0, 4, step, 0)
 
-    x_stage(6)
+    use_block(True, 5)
+    x_stage(6, True)
+    use_block(True, 6)
     total = x_sum(7)
-    wait(ZR.at[pl.ds(0, 7)], zs_r)
-    for d in range(1, 8):
-        total = total + ZR[lax.rem(z + d, 8)].astype(F32)
+    for n in (5, 6):
+        wait(ZR.at[n], zs_r.at[n])
+        total = total + ZR[n].astype(F32)
     my_piece = pl.ds(pl.multiple_of((y * 2 + X) * 32, 32), 32)
     RR[my_piece, :] = (total * (1.0 / math.sqrt(32768.0))).astype(BF16)
     for XX in (1 - X, X):
@@ -295,11 +310,7 @@
             to = dev(X=XX, y=(y + d) % 4)
             send(RR.at[my_piece], RR.at[my_piece], rr_s, rr_r, to)
 
-    def last(m, _):
-        use_block(True, m)
-        return 0
-
-    lax.fori_loop(5, 8, last, 0)
+    use_block(True, 7)
     send(PA.at[pl.ds(pl.multiple_of(oc * 128, 128), 128)], PR, pa_s, pa_r, peer)
 
     wait(PR, pa_r)
@@ -312,14 +323,14 @@
     wait(CA.at[pl.ds(0, 7)], ca_s)
     wait(TW.at[:, :, :, pl.ds(0, 896)], tw_s)
     wait(W.at[pl.ds(0, 7)], az_s)
-    wait(W.at[pl.ds(0, 7), pl.ds(0, 64)], bz_s)
+    wait(W.at[pl.ds(0, 7), pl.ds(0, 96)], bz_s)
     wait(W.at[0], ao_s)
-    wait(W.at[pl.ds(0, 7), pl.ds(0, 192)], ax_s)
+    wait(W.at[pl.ds(0, 7), pl.ds(0, 160)], ax_s)
     wait(XR, gx_s)
     wait(PR, pa_s)
 
     wait(ZS, zs_s)
-    wait(ZR.at[pl.ds(0, 7)], rr_s)
+    wait(ZR, rr_s)
     wait(half_tokens, ig_s)
     wait(half_tokens, ig_l)
     wait(half_tokens, ig_r)
@@ -375,7 +386,7 @@
             pltpu.VMEM((8, 128, 512), BF16),
             pltpu.VMEM((8, 3, 32, 512), BF16),
             pltpu.VMEM((7, 32, 512), BF16),
-            pltpu.VMEM((8, 32, 512), BF16),
+            pltpu.VMEM((7, 32, 512), BF16),
             pltpu.VMEM((256, 512), BF16),
             pltpu.VMEM((16, 256, 256), BF16),
             pltpu.VMEM((256, 512), F32),
@@ -392,7 +403,7 @@
             dma, dma((8, 2)),
             dma, dma, dma,
             dma, dma((8,)),
-            dma, dma,
+            dma, dma((7,)),
             dma, dma,
             dma, dma,
         ],

time: 60.5 us -> 58.9 us (0.974); the launches traced: 60.3 us -> 58 us
  Pallas kernels: 59.7 us -> 57.3 us
    pallas_call x1, Pallas kernels: 57 us -> 54.7 us  [body(): pl.pallas_call(kernel, out_shape=shapes, in_specs=[anywhere] * 5, out_spe...]
where the time goes in v4:
time: 58.9 us; the launch traced here: 58 us
  Pallas kernels  57.3 us (97%)
  between operations  0.64 us (1%)
    pallas_call x1, Pallas kernels, body(): pl.pallas_call(kernel, out_shape=shapes, in_specs=[anywhere] * 5, out_spe...  54.7 us
    pallas_call x1, Pallas kernels, body(): pl.pallas_call(finish, out_shape=shapes, in_specs=[anywhere] * 3, out_spe...  2.66 us

profile of v4, /device:TPU:1, one launch (start us, length us, event | category | flops | bytes accessed | tf_op | source)
XLA Modules:
  0.0 58.0 jit_solution(13853864386934794492)
XLA Ops:
  0.6 54.7 %shard_map.76 = (bf16[128,512]{1,0:T(8,128)(2,1)}, bf16[128,8192]{1,0:T(8,128)(2,1)}, f32[256,512]{1,0:T(8,128)}) custom-call(bf16[128,8192]{1,0:T(8,128)(2,1)} %tok.1, bf16[128,512]{1,0:T(8,128)(2,1)} %cot.1, bf16[8192,512]{1,0:T(8,128)(2,1)} %base.1, s32[256,512]{1,0:T(8,128)} %codes.1, f32[4,256]{1,0:T(4,128)} %bitcast.1), custom_call_target="tpu_custom_call" | custom-call | flops 3221225472 | bytes 25165824 | tf_op jit(solution)/shard_map/pallas_call | solution.py:368
  55.3 2.7 %shard_map.77 = (bf16[128,512]{1,0:T(8,128)(2,1)}, bf16[128,8192]{1,0:T(8,128)(2,1)}, f32[256,512]{1,0:T(8,128)}) custom-call(bf16[128,512]{1,0:T(8,128)(2,1)} %get-tuple-element.6.p_in, bf16[128,8192]{1,0:T(8,128)(2,1)} %get-tuple-element.7.i_in, f32[256,512]{1,0:T(8,128)} %get-tuple-element.8.w_in), custom_call_target="tpu_custom_call" | custom-call | tf_op jit(solution)/shard_map/pallas_call | solution.py:417

commit v5 on v4

--- a/solution.py
+++ b/solution.py
@@ -14,7 +14,7 @@
 def kernel(
     tok, cot, base, codes, scales,
     proj, igrad, wgrad,
-    W, BASE, TOK, TT, TK, CA, TW, GF, GX, XR, ZS, ZR, RR, IG, PA, PR, CO, SC,
+    W, BASE, TOK, TT, TK, CA, TW, GF, GX, XR, ZS, ZR, RR, IG, PA, PR, PJ, CO, SC,
     ld, tk_l, tk_s, tk_r, ca_s, ca_r, tw_s, tw_r, az_s, az_r, bz_s, bz_r, ao_s, ax_s, ax_r,
     ig_l, ig_s, ig_r, gx_s, gx_r, zs_s, zs_r, rr_s, rr_r, pa_s, pa_r,
 ):
@@ -37,34 +37,22 @@
     def send(src, dst, ssem, rsem, to):
         pltpu.make_async_remote_copy(src, dst, ssem, rsem, device_id=to).start()
 
+    barrier = pltpu.get_barrier_semaphore()
+    peers = [dev(X=1 - X, y=(y + d) % 4) for d in (2, 1, 3)]
+    peers += [dev(y=(y + d) % 4, c=cc) for d in (2, 1, 3) for cc in (c, oc)]
+    peers += [up, down]
+    peers += [O, A, B, peer]
+    for d in peers:
+        pl.semaphore_signal(barrier, 1, device_id=d)
+
     pltpu.make_async_copy(tok, TOK, ld.at[3]).start()
     pltpu.make_async_copy(codes, CO, ld.at[0]).start()
     pltpu.make_async_copy(scales, SC, ld.at[1]).start()
     me8 = y * 2 + c
     pltpu.make_async_copy(cot, CA.at[me8], ca_r.at[me8]).start()
 
-    barrier = pltpu.get_barrier_semaphore()
-    peers = [peer]
-    peers += [dev(y=(y + d) % 4, c=cc) for d in (1, 2, 3) for cc in (c, oc)]
-    peers += [up, down]
-    peers += [A, B, O]
-    peers += [dev(X=1 - X, y=(y + d) % 4) for d in (1, 2, 3)]
-    for d in peers:
-        pl.semaphore_signal(barrier, 1, device_id=d)
-
     def col(block, core):
         return pl.multiple_of((block * 2 + core) * 256, 256)
-
-    def load_block(b, _):
-        rows = pl.ds(col(b, c), 256)
-        pltpu.make_async_copy(base.at[rows], BASE.at[b], ld.at[2]).start()
-        dst = pl.ds(pl.multiple_of(b * 256, 256), 256)
-        pltpu.make_async_copy(
-            tok.at[:, rows], TK.at[pl.ds(c * 128, 128), dst], tk_l
-        ).start()
-        return 0
-
-    lax.fori_loop(0, 16, load_block, 0)
 
     def zof(n):
         return lax.rem(z + jnp.where(n % 2 == 1, 8 - (7 - n) // 2, 4 - n // 2), 8)
@@ -87,10 +75,10 @@
         send(half(block, h), half(block, h), az_s, az_r.at[t, way, h], (up, down)[way])
 
     def few(block, h):
-        return W.at[block, pl.ds(h * 128, 48)]
+        return W.at[block, pl.ds(h * 128, 64)]
 
     def most(block, h):
-        return W.at[block, pl.ds(h * 128 + 48, 80)]
+        return W.at[block, pl.ds(h * 128 + 64, 64)]
 
     def send_few(block, t, way, h):
         send(few(block, h), few(block, h), bz_s, bz_r.at[t, way, h], (up, down)[way])
@@ -137,6 +125,16 @@
     for n in range(4):
         turn(n)
         send_part(n)
+    def load_block(b, _):
+        rows = pl.ds(col(b, c), 256)
+        pltpu.make_async_copy(base.at[rows], BASE.at[b], ld.at[2]).start()
+        dst = pl.ds(pl.multiple_of(b * 256, 256), 256)
+        pltpu.make_async_copy(
+            tok.at[:, rows], TK.at[pl.ds(c * 128, 128), dst], tk_l
+        ).start()
+        return 0
+
+    lax.fori_loop(0, 16, load_block, 0)
     lax.fori_loop(0, 16, send_tokens, 0)
 
     PA[...] = jnp.zeros_like(PA)
@@ -152,7 +150,7 @@
 
     def use_block(other, m):
         zz = lax.rem(z + offset(m), 8)
-        block = jnp.where(other, 1 - l, l) * 8 + zz
+        block = (1 - l if other is True else l if other is False else jnp.where(other, 1 - l, l)) * 8 + zz
 
         def arrive():
             for h in range(2):
@@ -160,7 +158,7 @@
 
         if other is True:
             arrive()
-        else:
+        elif other is not False:
             pl.when(jnp.logical_and(other, m > 0))(arrive)
 
         w = (BASE[block].astype(F32) + W[block].astype(F32)).astype(BF16)
@@ -222,81 +220,98 @@
             def _():
                 ZS[n] = total.astype(BF16)
 
-        send(ZS.at[n], ZR.at[n], zs_s, zs_r.at[n], up if even else down)
+        to = dev(z=(z + jnp.where(even, 1, 7)) % 8)
+        send(ZS.at[n], ZR.at[n], zs_s, zs_r.at[n], to)
 
     beside = (1 - l) * 8 + z
 
-    def step(i, _):
-        t = i
-
-        @pl.when(t == 0)
-        def _():
-            for h in range(2):
-                wait(half(beside, h), ax_r.at[z, h])
-                send_few(beside, 0, 0, h)
-                send_few(beside, 0, 1, h)
-
-        zu, zd = lax.rem(z + 7 - t, 8), lax.rem(z + t + 1, 8)
+    def around(t):
+        return (0, lax.rem(z + 7 - t, 8)), (1, lax.rem(z + t + 1, 8))
+
+    def goes_on(t, h, way):
+        return jnp.logical_or(t < 2, jnp.logical_and(t == 2, h == way))
+
+    def gather_half(t, h):
+        for way, zz in around(t):
+            block = l * 8 + zz
+
+            @pl.when(jnp.logical_or(t < 3, h == way))
+            def _():
+                wait(half(block, h), az_r.at[t, way, h])
+                pl.when(goes_on(t, h, way))(lambda: send_z(block, t + 1, way, h))
+                send_x(block, zz, h)
+
+    def gather_few(t):
         for h in range(2):
-            for way, zz in ((0, zu), (1, zd)):
-                block = l * 8 + zz
+            for way, zz in around(t):
+                block = (1 - l) * 8 + zz
 
                 @pl.when(jnp.logical_or(t < 3, h == way))
                 def _():
-                    wait(half(block, h), az_r.at[t, way, h])
-
-                    @pl.when(jnp.logical_or(t < 2, jnp.logical_and(t == 2, h == way)))
-                    def _():
-                        send_z(block, t + 1, way, h)
-
-                    send_x(block, zz, h)
-
-        for h in range(2):
-            for way, zz in ((0, zu), (1, zd)):
-                block2 = (1 - l) * 8 + zz
-
-                @pl.when(jnp.logical_or(t < 3, h == way))
-                def _():
-                    wait(few(block2, h), bz_r.at[t, way, h])
-
-                    @pl.when(jnp.logical_or(t < 2, jnp.logical_and(t == 2, h == way)))
-                    def _():
-                        send_few(block2, t + 1, way, h)
-
-        @pl.when(i < 2)
-        def _():
-            for e in range(2):
-                turn(2 * i + 4 + e)
-                send_part(2 * i + 4 + e)
-
-        lo1 = jnp.where(i == 0, 0, 2 * i + 1)
-        n1 = jnp.minimum(2 * i + 3, 8) - lo1
-        lo2 = jnp.maximum(2 * i - 3, 0)
-        n2 = jnp.maximum(2 * i - 1, 0) - lo2
-
-        def one(n, _):
-            other = n >= n1
-            use_block(other, jnp.where(other, lo2 + n - n1, lo1 + n))
+                    wait(few(block, h), bz_r.at[t, way, h])
+                    pl.when(goes_on(t, h, way))(lambda: send_few(block, t + 1, way, h))
+
+    for h in range(2):
+        wait(half(beside, h), ax_r.at[z, h])
+        send_few(beside, 0, 0, h)
+        send_few(beside, 0, 1, h)
+
+    def pick(n, table):
+        value = jnp.int32(0)
+        for at, v in table.items():
+            value = jnp.where(n == at, v, value)
+        return value
+
+    def among(n, places):
+        return sum((n == at).astype(jnp.int32) for at in places) > 0
+
+    def step(n, _):
+        @pl.when(among(n, H0))
+        def _():
+            gather_half(pick(n, H0), 0)
+
+        @pl.when(among(n, H1))
+        def _():
+            gather_half(pick(n, H1), 1)
+
+        @pl.when(among(n, FEW))
+        def _():
+            gather_few(pick(n, FEW))
+
+        @pl.when(n < 4)
+        def _():
+            turn(n + 4)
+            send_part(n + 4)
+
+        other, first = among(n, (1, 2, 6)), pick(n, FIRST)
+
+        def one(q, _):
+            use_block(other, first + q)
             return 0
 
-        lax.fori_loop(0, n1 + n2, one, 0)
-
-        for e in range(2):
-            n = 2 * i + e
-
-            @pl.when(i > 0)
-            def _():
-                x_stage(n - 2, e == 0)
-
-            part(n)
+        lax.fori_loop(0, pick(n, COUNT), one, 0)
+        part(n)
+
+        @pl.when(n >= 2)
+        def _():
+            x_stage(n - 2, n % 2 == 0)
 
         return 0
 
-    lax.fori_loop(0, 4, step, 0)
-
+    H0 = {0: 0, 2: 1, 4: 2}
+    H1 = {0: 0, 3: 1, 5: 2}
+    FEW = {1: 0, 3: 1, 6: 2}
+    FIRST = {0: 0, 1: 0, 2: 1, 4: 3, 6: 3, 7: 5}
+    COUNT = {0: 3, 1: 1, 2: 2, 4: 2, 6: 2, 7: 2}
+
+    lax.fori_loop(0, 8, step, 0)
+
+    for h in range(2):
+        gather_half(jnp.int32(3), h)
+    use_block(False, 7)
+    x_stage(6, True)
+    gather_few(3)
     use_block(True, 5)
-    x_stage(6, True)
-    use_block(True, 6)
     total = x_sum(7)
     for n in (5, 6):
         wait(ZR.at[n], zs_r.at[n])
@@ -310,48 +325,56 @@
             to = dev(X=XX, y=(y + d) % 4)
             send(RR.at[my_piece], RR.at[my_piece], rr_s, rr_r, to)
 
+    use_block(True, 6)
     use_block(True, 7)
     send(PA.at[pl.ds(pl.multiple_of(oc * 128, 128), 128)], PR, pa_s, pa_r, peer)
 
     wait(PR, pa_r)
-    proj[...] = (PA[pl.ds(pl.multiple_of(c * 128, 128), 128), :] + PR[...]).astype(BF16)
+    PJ[...] = (PA[pl.ds(pl.multiple_of(c * 128, 128), 128), :] + PR[...]).astype(BF16)
+    pltpu.make_async_copy(PJ, proj, ld.at[0]).start()
 
     wait(RR.at[pl.ds(0, 224)], rr_r)
-    wgrad[...] = RR[...].astype(F32)
+    pltpu.make_async_copy(RR, wgrad, ld.at[1]).start()
 
     wait(half_tokens, tk_s)
     wait(CA.at[pl.ds(0, 7)], ca_s)
     wait(TW.at[:, :, :, pl.ds(0, 896)], tw_s)
     wait(W.at[pl.ds(0, 7)], az_s)
-    wait(W.at[pl.ds(0, 7), pl.ds(0, 96)], bz_s)
+    wait(W.at[pl.ds(0, 7), pl.ds(0, 128)], bz_s)
     wait(W.at[0], ao_s)
-    wait(W.at[pl.ds(0, 7), pl.ds(0, 160)], ax_s)
+    wait(W.at[pl.ds(0, 7), pl.ds(0, 128)], ax_s)
     wait(XR, gx_s)
     wait(PR, pa_s)
 
     wait(ZS, zs_s)
     wait(ZR, rr_s)
+    wait(PJ, ld.at[0])
     wait(half_tokens, ig_s)
     wait(half_tokens, ig_l)
     wait(half_tokens, ig_r)
-
-
-def finish(p_in, i_in, w_in, p_out, i_out, w_out, p_buf, i_buf, w_buf, sem_in, sem_out):
-    pieces = [(w_in, w_buf, w_out)]
-    pieces += [
-        tuple(ref.at[pl.ds(n * 32, 32)] for ref in (i_in, i_buf, i_out)) for n in range(4)
-    ]
-    pieces += [(p_in, p_buf, p_out)]
+    wait(RR, ld.at[1])
+
+
+def finish(p_in, i_in, w_in, p_out, i_out, w_out, p_buf, i_buf, w_half, w_buf, sem_in, sem_out):
+    pieces = [(w_in, w_half, w_buf, w_out)]
+    for n in range(4):
+        rows = pl.ds(n * 32, 32)
+        pieces.append((i_in.at[rows], i_buf.at[rows], i_buf.at[rows], i_out.at[rows]))
+    pieces.append((p_in, p_buf, p_buf, p_out))
     loads = [
-        pltpu.make_async_copy(src, buf, sem_in.at[n]) for n, (src, buf, _) in enumerate(pieces)
+        pltpu.make_async_copy(src, buf, sem_in.at[n])
+        for n, (src, buf, _, _) in enumerate(pieces)
     ]
     stores = [
-        pltpu.make_async_copy(buf, dst, sem_out.at[n]) for n, (_, buf, dst) in enumerate(pieces)
+        pltpu.make_async_copy(buf, dst, sem_out.at[n])
+        for n, (_, _, buf, dst) in enumerate(pieces)
     ]
     for load in loads:
         load.start()
-    for load, store in zip(loads, stores):
+    for n, (load, store) in enumerate(zip(loads, stores)):
         load.wait()
+        if n == 0:
+            w_buf[...] = w_half[...].astype(F32)
         store.start()
     for store in stores:
         store.wait()
@@ -360,20 +383,18 @@
 def body(tokens, cotangent, base_copy, codes, scales):
     dma = pltpu.SemaphoreType.DMA
     anywhere = pl.BlockSpec(memory_space=pl.ANY)
-    shapes = (
-        jax.ShapeDtypeStruct((128, 512), BF16),
-        jax.ShapeDtypeStruct((128, 8192), BF16),
-        jax.ShapeDtypeStruct((256, 512), F32),
-    )
+    def shapes(of_weight):
+        return (
+            jax.ShapeDtypeStruct((128, 512), BF16),
+            jax.ShapeDtypeStruct((128, 8192), BF16),
+            jax.ShapeDtypeStruct((256, 512), of_weight),
+        )
+
     results = pl.pallas_call(
         kernel,
-        out_shape=shapes,
+        out_shape=shapes(BF16),
         in_specs=[anywhere] * 5,
-        out_specs=(
-            pl.BlockSpec(memory_space=pltpu.VMEM),
-            anywhere,
-            pl.BlockSpec(memory_space=pltpu.VMEM),
-        ),
+        out_specs=(anywhere,) * 3,
         scratch_shapes=[
             pltpu.VMEM((16, 256, 512), BF16),
             pltpu.VMEM((16, 256, 512), BF16),
@@ -391,6 +412,7 @@
             pltpu.VMEM((16, 256, 256), BF16),
             pltpu.VMEM((256, 512), F32),
             pltpu.VMEM((128, 512), F32),
+            pltpu.VMEM((128, 512), BF16),
             pltpu.VMEM((256, 512), jnp.int32),
             pltpu.VMEM((4, 256), F32),
             dma((4,)),
@@ -416,12 +438,13 @@
     )(tokens, cotangent, base_copy, codes, scales.T)
     return pl.pallas_call(
         finish,
-        out_shape=shapes,
+        out_shape=shapes(F32),
         in_specs=[anywhere] * 3,
         out_specs=(anywhere,) * 3,
         scratch_shapes=[
             pltpu.VMEM((128, 512), BF16),
             pltpu.VMEM((128, 8192), BF16),
+            pltpu.VMEM((256, 512), BF16),
             pltpu.VMEM((256, 512), F32),
             dma((6,)),
             dma((6,)),

time: 58.9 us -> 56.9 us (0.966); the launches traced: 58 us -> 56.7 us
  Pallas kernels: 57.3 us -> 56 us
    pallas_call x2, Pallas kernels: 57.3 us -> 56 us  [the longest x1 53.4 us: body(): pl.pallas_call(kernel, out_shape=shapes(BF16), in_specs=[anywhere] * 5, o...]
where the time goes in v5:
time: 56.9 us; the launch traced here: 56.7 us
  Pallas kernels  56 us (98%)
  between operations  0.64 us (1%)
    pallas_call x1, Pallas kernels, body(): pl.pallas_call(kernel, out_shape=shapes(BF16), in_specs=[anywhere] * 5, o...  53.4 us
    pallas_call x1, Pallas kernels, body(): pl.pallas_call(finish, out_shape=shapes(F32), in_specs=[anywhere] * 3, ou...  2.61 us

profile of v5, /device:TPU:1, one launch (start us, length us, event | category | flops | bytes accessed | tf_op | source)
XLA Modules:
  0.0 56.7 jit_solution(14751895364965013809)
XLA Ops:
  0.6 53.4 %shard_map.76 = (bf16[128,512]{1,0:T(8,128)(2,1)}, bf16[128,8192]{1,0:T(8,128)(2,1)}, bf16[256,512]{1,0:T(8,128)(2,1)}) custom-call(bf16[128,8192]{1,0:T(8,128)(2,1)} %tok.1, bf16[128,512]{1,0:T(8,128)(2,1)} %cot.1, bf16[8192,512]{1,0:T(8,128)(2,1)} %base.1, s32[256,512]{1,0:T(8,128)} %codes.1, f32[4,256]{1,0:T(4,128)} %bitcast.1), custom_call_target="tpu_custom_call" | custom-call | flops 3221225472 | bytes 25165824 | tf_op jit(solution)/shard_map/pallas_call | solution.py:393
  54.1 2.6 %shard_map.77 = (bf16[128,512]{1,0:T(8,128)(2,1)}, bf16[128,8192]{1,0:T(8,128)(2,1)}, f32[256,512]{1,0:T(8,128)}) custom-call(bf16[128,512]{1,0:T(8,128)(2,1)} %get-tuple-element.6.p_in, bf16[128,8192]{1,0:T(8,128)(2,1)} %get-tuple-element.7.i_in, bf16[256,512]{1,0:T(8,128)(2,1)} %get-tuple-element.8.w_in), custom_call_target="tpu_custom_call" | custom-call | tf_op jit(solution)/shard_map/pallas_call | solution.py:439

commit v6 on v5

--- a/solution.py
+++ b/solution.py
@@ -300,7 +300,7 @@
 
     H0 = {0: 0, 2: 1, 4: 2}
     H1 = {0: 0, 3: 1, 5: 2}
-    FEW = {1: 0, 3: 1, 6: 2}
+    FEW = {1: 0, 4: 1, 7: 2}
     FIRST = {0: 0, 1: 0, 2: 1, 4: 3, 6: 3, 7: 5}
     COUNT = {0: 3, 1: 1, 2: 2, 4: 2, 6: 2, 7: 2}
 

time: 56.9 us -> 56.4 us (level)
  no operation moved by 1% of the time
where the time goes in v6:
time: 56.4 us; the launch traced here: 56.2 us
  Pallas kernels  55.5 us (98%)
  between operations  0.64 us (1%)
    pallas_call x1, Pallas kernels, body(): pl.pallas_call(kernel, out_shape=shapes(BF16), in_specs=[anywhere] * 5, o...  52.9 us
    pallas_call x1, Pallas kernels, body(): pl.pallas_call(finish, out_shape=shapes(F32), in_specs=[anywhere] * 3, ou...  2.61 us

profile of v6, /device:TPU:1, one launch (start us, length us, event | category | flops | bytes accessed | tf_op | source)
XLA Modules:
  0.0 56.2 jit_solution(7739859785111624624)
XLA Ops:
  0.6 52.9 %shard_map.76 = (bf16[128,512]{1,0:T(8,128)(2,1)}, bf16[128,8192]{1,0:T(8,128)(2,1)}, bf16[256,512]{1,0:T(8,128)(2,1)}) custom-call(bf16[128,8192]{1,0:T(8,128)(2,1)} %tok.1, bf16[128,512]{1,0:T(8,128)(2,1)} %cot.1, bf16[8192,512]{1,0:T(8,128)(2,1)} %base.1, s32[256,512]{1,0:T(8,128)} %codes.1, f32[4,256]{1,0:T(4,128)} %bitcast.1), custom_call_target="tpu_custom_call" | custom-call | flops 3221225472 | bytes 25165824 | tf_op jit(solution)/shard_map/pallas_call | solution.py:393
  53.5 2.6 %shard_map.77 = (bf16[128,512]{1,0:T(8,128)(2,1)}, bf16[128,8192]{1,0:T(8,128)(2,1)}, f32[256,512]{1,0:T(8,128)}) custom-call(bf16[128,512]{1,0:T(8,128)(2,1)} %get-tuple-element.6.p_in, bf16[128,8192]{1,0:T(8,128)(2,1)} %get-tuple-element.7.i_in, bf16[256,512]{1,0:T(8,128)(2,1)} %get-tuple-element.8.w_in), custom_call_target="tpu_custom_call" | custom-call | tf_op jit(solution)/shard_map/pallas_call | solution.py:439

commit v7 on v6

--- a/solution.py
+++ b/solution.py
@@ -323,7 +323,8 @@
             if XX is X and d == 0:
                 continue
             to = dev(X=XX, y=(y + d) % 4)
-            send(RR.at[my_piece], RR.at[my_piece], rr_s, rr_r, to)
+            send(RR.at[my_piece], wgrad.at[my_piece], rr_s, rr_r, to)
+    pltpu.make_async_copy(RR.at[my_piece], wgrad.at[my_piece], ld.at[1]).start()
 
     use_block(True, 6)
     use_block(True, 7)
@@ -332,9 +333,6 @@
     wait(PR, pa_r)
     PJ[...] = (PA[pl.ds(pl.multiple_of(c * 128, 128), 128), :] + PR[...]).astype(BF16)
     pltpu.make_async_copy(PJ, proj, ld.at[0]).start()
-
-    wait(RR.at[pl.ds(0, 224)], rr_r)
-    pltpu.make_async_copy(RR, wgrad, ld.at[1]).start()
 
     wait(half_tokens, tk_s)
     wait(CA.at[pl.ds(0, 7)], ca_s)
@@ -352,7 +350,8 @@
     wait(half_tokens, ig_s)
     wait(half_tokens, ig_l)
     wait(half_tokens, ig_r)
-    wait(RR, ld.at[1])
+    wait(RR.at[my_piece], ld.at[1])
+    wait(RR.at[pl.ds(0, 224)], rr_r)
 
 
 def finish(p_in, i_in, w_in, p_out, i_out, w_out, p_buf, i_buf, w_half, w_buf, sem_in, sem_out):

time: 56.4 us -> 56.2 us (level)
  no operation moved by 1% of the time
where the time goes in v7:
time: 56.2 us; the launch traced here: 56 us
  Pallas kernels  55.4 us (99%)
  between operations  0.64 us (1%)
    pallas_call x1, Pallas kernels, body(): pl.pallas_call(kernel, out_shape=shapes(BF16), in_specs=[anywhere] * 5, o...  52.8 us
    pallas_call x1, Pallas kernels, body(): pl.pallas_call(finish, out_shape=shapes(F32), in_specs=[anywhere] * 3, ou...  2.61 us

profile of v7, /device:TPU:1, one launch (start us, length us, event | category | flops | bytes accessed | tf_op | source)
XLA Modules:
  0.0 56.0 jit_solution(658069295248152176)
XLA Ops:
  0.6 52.8 %shard_map.76 = (bf16[128,512]{1,0:T(8,128)(2,1)}, bf16[128,8192]{1,0:T(8,128)(2,1)}, bf16[256,512]{1,0:T(8,128)(2,1)}) custom-call(bf16[128,8192]{1,0:T(8,128)(2,1)} %tok.1, bf16[128,512]{1,0:T(8,128)(2,1)} %cot.1, bf16[8192,512]{1,0:T(8,128)(2,1)} %base.1, s32[256,512]{1,0:T(8,128)} %codes.1, f32[4,256]{1,0:T(4,128)} %bitcast.1), custom_call_target="tpu_custom_call" | custom-call | flops 3221225472 | bytes 25165824 | tf_op jit(solution)/shard_map/pallas_call | solution.py:392
  53.4 2.6 %shard_map.77 = (bf16[128,512]{1,0:T(8,128)(2,1)}, bf16[128,8192]{1,0:T(8,128)(2,1)}, f32[256,512]{1,0:T(8,128)}) custom-call(bf16[128,512]{1,0:T(8,128)(2,1)} %get-tuple-element.6.p_in, bf16[128,8192]{1,0:T(8,128)(2,1)} %get-tuple-element.7.i_in, bf16[256,512]{1,0:T(8,128)(2,1)} %get-tuple-element.8.w_in), custom_call_target="tpu_custom_call" | custom-call | tf_op jit(solution)/shard_map/pallas_call | solution.py:438
